TPU v7x, 128 devices: a whole 4x4x4 slice. The times are simulated.
128 devices in a mesh: tm: 16 (over x, y), sy: 4 (over z), sx: 2 (over core).
Axes of the slice: x: 4, y: 4, z: 4, core: 2. Of those that a mesh axis runs over, the one named last changes fastest.
Arguments:
- latent: bfloat16 [32, 128, 64, 16], P('tm', 'sy', 'sx'), may hold values from -6 to 6
- clip_lengths: int32 [9], replicated, may hold values from 1 to 16, as said below
- entry_kernel: bfloat16 [3, 3, 3, 16, 384], replicated, may hold values from -0.3125 to 0.3125
- first_gain: float32 [384], replicated, may hold values from 0.25 to 1.75
- first_kernel: bfloat16 [3, 3, 3, 384, 384], replicated, may hold values from -0.0625 to 0.0625
- second_gain: float32 [384], replicated, may hold values from 0.25 to 1.75
- second_kernel: bfloat16 [3, 3, 3, 384, 384], replicated, may hold values from -0.0625 to 0.0625
Outputs:
- decoded: bfloat16 [32, 128, 64, 384], P('tm', 'sy', 'sx')
Inputs may be any that keep to these rules, and one draw needn't show every extreme that they name: `clip_lengths`: 9 clips packed in order; their lengths sum to 32; the last clip is the longest, with exactly 16 frames.
All inputs are finite; a program needn't handle non-finite values.
Results may differ from a plain program's by a relative error of at most 0.015.
Values may be sent and summed in bfloat16 or wider, within the bound.
A program may use at most 192 MiB of HBM per device.

v0:
```python
import functools

import jax
import jax.numpy as jnp
from jax import lax
from jax.experimental import pallas as pl
from jax.experimental.pallas import tpu as pltpu
from jax.sharding import PartitionSpec as P

C = 384
K3 = 3 * C
MIB = 2**20
BF = jnp.bfloat16
F32 = jnp.float32


def passed_along(block, axis, distance):
    devices = range(lax.axis_size(axis))
    route = [(i - distance, i) for i in devices if i - distance in devices]
    return lax.ppermute(block, axis, route)


def padded(block, sides, width):
    for axis, dim in sides:
        count = lax.axis_size(axis)
        forward = [(i, i + 1) for i in range(count - 1)]
        backward = [(target, source) for source, target in forward]
        low = lax.ppermute(
            lax.slice_in_dim(block, block.shape[dim] - width, None, axis=dim), axis, forward
        )
        high = lax.ppermute(lax.slice_in_dim(block, 0, width, axis=dim), axis, backward)
        block = jnp.concatenate([low, block, high], axis=dim)
    return block


def clip_distance(clip_lengths, positions):
    starts = jnp.cumsum(clip_lengths) - clip_lengths
    earlier = starts[None, :] <= positions[:, None]
    latest = jnp.max(jnp.where(earlier, starts[None, :], -1), axis=1)
    return positions - latest


def weights_kernel(w_ref, u_ref):
    step = 16

    @pl.loop(0, w_ref.shape[3] // step)
    def _(block):
        part = pl.ds(pl.multiple_of(block * step, step), step)
        w = [[w_ref[t, y, 0, part, :].astype(F32) for y in range(3)] for t in range(3)]

        def rows(g, out):
            u_ref[out, 0, 0, part, :] = g[0].astype(BF)
            edge = g[0] + g[2]
            u_ref[out, 1, 0, part, :] = ((edge + g[1]) * 0.5).astype(BF)
            u_ref[out, 2, 0, part, :] = ((edge - g[1]) * 0.5).astype(BF)
            u_ref[out, 3, 0, part, :] = g[2].astype(BF)

        rows(w[0], 0)
        rows([(w[0][y] + w[2][y] + w[1][y]) * 0.5 for y in range(3)], 1)
        rows([(w[0][y] + w[2][y] - w[1][y]) * 0.5 for y in range(3)], 2)
        rows(w[2], 3)
        rows(w[1], 4)


def transformed_weights(kernel):
    chunk = 128
    return pl.pallas_call(
        weights_kernel,
        grid=(3, C // chunk),
        in_specs=[pl.BlockSpec((3, 3, 1, chunk, C), lambda x, c: (0, 0, x, c, 0))],
        out_specs=pl.BlockSpec((5, 4, 1, chunk, C), lambda x, c: (0, 0, x, c, 0)),
        out_shape=jax.ShapeDtypeStruct((5, 4, 3, C, C), BF),
        compiler_params=pltpu.CompilerParams(vmem_limit_bytes=32 * MIB),
        cost_estimate=pl.CostEstimate(
            flops=30 * 3 * C * C * 3, bytes_accessed=47 * 3 * C * C * 2, transcendentals=0
        ),
        name="weights",
    )(kernel).reshape(5, 4, K3, C)


ROWS = 32
COLS = 32
WIDE = 40
LEAD = 9
CELLS = 256
R1 = ROWS + 4
R2 = ROWS + 2
I1 = R2 // 2
I2 = ROWS // 2
M1 = I1 * COLS + 32
M2 = I2 * COLS
HALF = 24
ENTRY_ROWS = 4


def norm_act(values, gain, keep):
    mean = jnp.mean(values * values, axis=-1, keepdims=True)
    half = values * (lax.rsqrt(mean + 1e-6) * keep) * gain
    return half * jnp.tanh(half) + half


def splat(value, shape):
    one = jnp.full((16, 128), value, F32).astype(BF)
    return jnp.tile(one, (shape[0] // 16, shape[1] // 128))


def main_kernel(
    ints, coefs, q_ref, we_ref, keep_ref, g1_ref, g2_ref, u1_hbm, u2_hbm,
    out_ref,
    f_ref, h_ref, s_ref, e_ref, x_ref, m_ref, acc_ref, w_ref, a_ref, b_ref, hn_ref, sem,
):
    halo_place = ints[0]
    top = ints[1]
    bottom = ints[2]
    halo_slot = ints[3]
    zero_slot = ints[4]

    def fetch(step, slot, source=u1_hbm):
        which = ints[8 + step]
        return pltpu.make_async_copy(source.at[which], w_ref.at[slot], sem.at[slot])

    fetch(0, 0).start()

    h_ref[...] = jnp.zeros_like(h_ref)

    @pl.loop(0, R1 // ENTRY_ROWS)
    def _(block):
        cols = []
        for n in range(ENTRY_ROWS):
            first = pl.multiple_of((block * ENTRY_ROWS + n) * 16, 16)
            cols.append(
                jnp.concatenate([q_ref[k, pl.ds(first, 48), :] for k in range(9)], axis=0)
            )
        patches = jnp.concatenate(cols, axis=1)
        entry = lax.dot_general(
            patches, we_ref[...], (((0,), (0,)), ((), ())), preferred_element_type=F32
        ).astype(BF)
        for n in range(ENTRY_ROWS):
            row = block * ENTRY_ROWS + n
            inside = jnp.where(row < 2, top, jnp.where(row >= R1 - 2, bottom, 1)).astype(F32)
            value = entry[n * CELLS : (n + 1) * CELLS].astype(F32)
            b_ref[n] = value
            a_ref[n] = norm_act(value, g1_ref[...], keep_ref[...] * inside)
        for n in range(ENTRY_ROWS):
            row = block * ENTRY_ROWS + n
            for f in range(2):
                e_ref[f, row] = b_ref[n, pl.ds((4 + f) * WIDE + LEAD, COLS), :].astype(BF)
            for f in range(6):
                for dx in range(3):
                    lanes = slice(dx * C, (dx + 1) * C)
                    place = f * WIDE + LEAD - 1 + dx
                    f_ref[f, row, :, lanes] = a_ref[n, pl.ds(place, COLS), :].astype(BF)
                    h_ref[f, n % 2, pl.ds(row // 2, 1), lanes] = a_ref[
                        n, pl.ds(f * WIDE + halo_place + dx, 1), :
                    ]

    def products(step, slot, rows):
        for k in range(4):
            m_ref[k, :rows, :] = jnp.dot(
                x_ref[k, :rows, :], w_ref[slot, k], preferred_element_type=F32
            )
        first = coefs[step, 2]
        second = coefs[step, 3]

        @pl.loop(0, rows // COLS)
        def _(i):
            part = pl.ds(pl.multiple_of(i * COLS, COLS), COLS)
            terms = [m_ref[k, part, :] for k in range(4)]
            even = terms[0] + terms[1] + terms[2]
            odd = terms[1] - terms[2] - terms[3]
            for parity, value in enumerate((even, odd)):
                acc_ref[0, parity, part, :] += first * value
                acc_ref[1, parity, part, :] += second * value

    def row_transform(d):
        return d[0] - d[2], d[1] + d[2], d[2] - d[1], d[1] - d[3]

    def frames_of(tau, base):
        one = jnp.where(tau == 0, 0, jnp.where(tau == 2, 2, 1)) + base
        other = jnp.where(tau == 2, 1, jnp.where(tau == 3, 3, 2)) + base
        return one, other

    def build(source, rows, step, one, other):
        shape = (COLS, K3)
        c_one = splat(coefs[step, 0], shape)
        c_other = splat(coefs[step, 1], shape)

        @pl.loop(0, rows)
        def _(i):
            d = [
                c_one * source[one, 2 * i + k] + c_other * source[other, 2 * i + k]
                for k in range(4)
            ]
            for k, value in enumerate(row_transform(d)):
                x_ref[k, pl.ds(pl.multiple_of(i * COLS, COLS), COLS), :] = value

    @pl.loop(0, 8)
    def _(step):
        slot = lax.rem(step, 2)
        tau = lax.rem(step, 4)
        pair = step // 4
        fetch(step, slot).wait()

        @pl.when(step < 7)
        def _():
            fetch(step + 1, 1 - slot).start()

        @pl.when(step == 7)
        def _():
            fetch(step + 1, 1 - slot, u2_hbm).start()

        one, other = frames_of(tau, 2 * pair)
        build(f_ref, I1, step, one, other)
        d = []
        for k in range(4):
            part = pl.ds(k // 2, HALF)
            d.append(
                coefs[step, 0] * h_ref[one, k % 2, part, :]
                + coefs[step, 1] * h_ref[other, k % 2, part, :]
            )
        for k, value in enumerate(row_transform(d)):
            both = jnp.concatenate([value, jnp.zeros((32 - HALF, K3), F32)], axis=0)
            x_ref[k, I1 * COLS :, :] = both.astype(BF)

        @pl.when(tau == 0)
        def _():
            acc_ref[...] = jnp.zeros_like(acc_ref)

        products(step, slot, M1)

        @pl.when(tau == 3)
        def _():
            for member in range(2):
                frame = 2 * pair + member
                for parity in range(2):
                    hn_ref[parity] = norm_act(
                        acc_ref[member, parity, I1 * COLS :, :], g2_ref[...], 1.0
                    )

                @pl.loop(0, I1)
                def _(i):
                    for parity in range(2):
                        row = 2 * i + parity
                        inside = jnp.where(
                            row == 0, top, jnp.where(row == R2 - 1, bottom, 1)
                        ).astype(F32)
                        part = pl.ds(pl.multiple_of(i * COLS, COLS), COLS)
                        value = norm_act(acc_ref[member, parity, part, :], g2_ref[...], inside)
                        a_ref[parity, pl.ds(8, COLS), :] = value
                        a_ref[parity, pl.ds(halo_slot, 1), :] = (
                            hn_ref[parity, pl.ds(i, 1), :] * inside
                        )
                        a_ref[parity, pl.ds(zero_slot, 1), :] = jnp.zeros((1, C), F32)
                        for dx in range(3):
                            s_ref[frame, row, :, dx * C : (dx + 1) * C] = a_ref[
                                parity, pl.ds(7 + dx, COLS), :
                            ].astype(BF)

    acc_ref[...] = jnp.zeros_like(acc_ref)

    @pl.loop(8, 12)
    def _(step):
        slot = lax.rem(step, 2)
        tau = lax.rem(step, 4)
        fetch(step, slot, u2_hbm).wait()

        @pl.when(step < 11)
        def _():
            fetch(step + 1, 1 - slot, u2_hbm).start()

        one, other = frames_of(tau, 0)
        build(s_ref, I2, step, one, other)
        products(step, slot, M2)

    for member in range(2):

        @pl.loop(0, I2)
        def _(i):
            for parity in range(2):
                row = 2 * i + parity
                part = pl.ds(pl.multiple_of(i * COLS, COLS), COLS)
                out_ref[member, row] = (
                    acc_ref[member, parity, part, :] + e_ref[member, row + 2].astype(F32)
                ).astype(BF)


def body(latent, clip_lengths, entry_kernel, first_gain, first_kernel, second_gain, second_kernel):
    tm = lax.axis_index("tm")
    sy = lax.axis_index("sy")
    sx = lax.axis_index("sx")
    start = tm * 2

    earlier = [passed_along(latent, "tm", n) for n in (3, 2, 1)]
    window = padded(jnp.concatenate(earlier + [latent], 0), (("sy", 1), ("sx", 2)), 3)
    u1 = transformed_weights(first_kernel)
    u2 = transformed_weights(second_kernel)

    across = jnp.transpose(window, (1, 3, 0, 2))
    across = jnp.pad(across, ((0, 0), (0, 0), (0, 0), (0, WIDE - 38))).reshape(38 * 16, 8 * WIDE)
    across = jnp.pad(across, ((0, 0), (LEAD + 1 - 3, 384 - 8 * WIDE - (LEAD + 1 - 3))))

    positions = start - 4 + jnp.arange(6, dtype=jnp.int32)
    distance = clip_distance(clip_lengths, positions)
    place = jnp.arange(CELLS)
    frame_of = jnp.clip((place - (LEAD - 4)) // WIDE, 0, 5)
    column_of = place - LEAD - frame_of * WIDE
    pieces = []
    for lag in range(3):
        mask = (distance >= lag)[frame_of].astype(BF)
        for dx in range(3):
            first = (2 - lag) * WIDE + dx
            pieces.append(across[:, first : first + CELLS] * mask[None, :])
    q = jnp.stack(pieces)
    we = jnp.transpose(entry_kernel[::-1], (0, 2, 1, 3, 4)).reshape(432, C)

    low = jnp.where(sx == 0, 0, -2)
    high = jnp.where(sx == 0, COLS + 2, COLS)
    keep = ((column_of >= low) & (column_of < high)).astype(F32)[:, None]

    ints = []
    ints.append(jnp.where(sx == 0, COLS, -1) + LEAD - 1)
    ints.append((sy > 0).astype(jnp.int32))
    ints.append((sy < lax.axis_size("sy") - 1).astype(jnp.int32))
    ints.append(jnp.where(sx == 0, 8 + COLS, 7))
    ints.append(jnp.where(sx == 0, 7, 8 + COLS))
    ints += [0, 0, 0]
    coefs = []
    for pair in (0, 1, 1):
        da = distance[2 + 2 * pair]
        db = distance[3 + 2 * pair]
        k0 = (da >= 2).astype(F32)
        k1 = (da >= 1).astype(F32)
        s = (db >= 1).astype(F32)
        whole = db >= 1
        coefs += [
            [k0, -s, 1.0, 0.0],
            [k1, s, 1.0, s],
            [1.0, -s * k1, 1.0, -s],
            [s * k1, -1.0, 0.0, -1.0],
        ]
        ints += [0, jnp.where(whole, 1, 4), jnp.where(whole, 2, 3), 3]
    ints = jnp.stack([jnp.asarray(v, jnp.int32) for v in ints])
    coefs = jnp.stack([jnp.stack([jnp.asarray(v, F32) for v in line]) for line in coefs])

    vmem = pl.BlockSpec(memory_space=pltpu.VMEM)
    smem = pl.BlockSpec(memory_space=pltpu.SMEM)
    hbm = pl.BlockSpec(memory_space=pl.ANY)
    return pl.pallas_call(
        main_kernel,
        in_specs=[smem, smem, vmem, vmem, vmem, vmem, vmem, hbm, hbm],
        out_specs=vmem,
        out_shape=jax.ShapeDtypeStruct((2, ROWS, COLS, C), BF),
        scratch_shapes=[
            pltpu.VMEM((6, R1, COLS, K3), BF),
            pltpu.VMEM((6, 2, HALF + 8, K3), F32),
            pltpu.VMEM((4, R2, COLS, K3), BF),
            pltpu.VMEM((2, R1, COLS, C), BF),
            pltpu.VMEM((4, M1, K3), BF),
            pltpu.VMEM((4, M1, C), F32),
            pltpu.VMEM((2, 2, M1, C), F32),
            pltpu.VMEM((2, 4, K3, C), BF),
            pltpu.VMEM((ENTRY_ROWS, CELLS, C), F32),
            pltpu.VMEM((ENTRY_ROWS, CELLS, C), F32),
            pltpu.VMEM((2, 32, C), F32),
            pltpu.SemaphoreType.DMA((2,)),
        ],
        compiler_params=pltpu.CompilerParams(vmem_limit_bytes=62 * MIB),
        name="block",
    )(
        ints, coefs, q, we, keep, first_gain[None, :] * 0.5, second_gain[None, :] * 0.5, u1, u2
    )


def solution(mesh):
    return jax.shard_map(
        body,
        mesh=mesh,
        in_specs=(P("tm", "sy", "sx", None), P(), P(), P(), P(), P(), P()),
        out_specs=P("tm", "sy", "sx", None),
        check_vma=False,
    )
```

profile of v0, /device:TPU:1, one launch (start us, length us, event | category | flops | bytes accessed | tf_op | source)
XLA Modules:
  0.0 175.9 jit_solution(5488473883428000980)
XLA Ops:
  0.0 5.7 %collective-permute-start.1 = (bf16[2,32,32,16]{2,3,1,0:T(8,128)(2,1)}, bf16[2,32,32,16]{2,3,1,0:T(8,128)(2,1)S(1)}, u32[]{:S(2)}, u32[]{:S(2)}) collective-permute-start(bf16[2,32,32,16]{2,3,1,0:T(8,128)(2,1)} %param.7), channel_id=1, source_target_pairs={{0,16},{8,24},{16,32},{24,40},{32,48},{40,56},{48,64},{56,72},{64,... | collective-permute-start | bytes 196616 | tf_op jit(solution)/shard_map/ppermute | solution.py:20
  5.7 3.6 %collective-permute-start = (bf16[2,32,32,16]{2,3,1,0:T(8,128)(2,1)}, bf16[2,32,32,16]{2,3,1,0:T(8,128)(2,1)S(1)}, u32[]{:S(2)}, u32[]{:S(2)}) collective-permute-start(bf16[2,32,32,16]{2,3,1,0:T(8,128)(2,1)} %param.7), channel_id=1, source_target_pairs={{0,24},{8,32},{16,40},{24,48},{32,56},{40,64},{48,72},{56,80},{64,... | collective-permute-start | bytes 196616 | tf_op jit(solution)/shard_map/ppermute | solution.py:20
  9.3 2.6 %collective-permute-start.2 = (bf16[2,32,32,16]{2,3,1,0:T(8,128)(2,1)}, bf16[2,32,32,16]{2,3,1,0:T(8,128)(2,1)S(1)}, u32[]{:S(2)}, u32[]{:S(2)}) collective-permute-start(bf16[2,32,32,16]{2,3,1,0:T(8,128)(2,1)} %param.7), channel_id=1, source_target_pairs={{0,8},{8,16},{16,24},{24,32},{32,40},{40,48},{48,56},{56,64},{64,7... | collective-permute-start | bytes 196616 | tf_op jit(solution)/shard_map/ppermute | solution.py:20
  11.9 0.8 reduce-window.9
  13.6 0.7 fusion.30
  18.1 0.7 broadcast_multiply_fusion.1
  18.8 0.7 broadcast_multiply_fusion
  19.5 0.7 fusion.27
  20.2 1.0 reverse_bitcast_fusion
  21.2 0.7 fusion.28
  21.9 0.7 and_convert_fusion.keep_ref
  24.1 0.8 copy.64
  24.9 1.2 stack.193.coefs
  26.1 0.7 stack.168.ints
  26.8 3.3 %copy-done = bf16[3,3,3,384,384]{4,3,2,1,0:T(8,128)(2,1)S(1)} copy-done((bf16[3,3,3,384,384]{4,3,2,1,0:T(8,128)(2,1)S(1)}, bf16[3,3,3,384,384]{4,3,2,1,0:T(8,128)(2,1)}, u32[]{:S(2)}) %copy-start) | copy-done | bytes 7962648
  30.0 9.2 %weights.2 = bf16[5,4,3,384,384]{4,3,2,1,0:T(8,128)(2,1)} custom-call(bf16[3,3,3,384,384]{4,3,2,1,0:T(8,128)(2,1)S(1)} %copy-done), custom_call_target="tpu_custom_call" | custom-call | flops 39813120 | bytes 41582592 | tf_op jit(solution)/shard_map/weights/pallas_call | solution.py:67
  39.3 9.2 %weights.3 = bf16[5,4,3,384,384]{4,3,2,1,0:T(8,128)(2,1)} custom-call(bf16[3,3,3,384,384]{4,3,2,1,0:T(8,128)(2,1)S(1)} %copy-done.1), custom_call_target="tpu_custom_call" | custom-call | flops 39813120 | bytes 41582592 | tf_op jit(solution)/shard_map/weights/pallas_call | solution.py:67
  48.5 4.0 %fusion.10 = bf16[256]{0:T(256)(128)(2,1)S(1)} fusion(pred[]{:T(512)} %bitcast.44, pred[]{:T(512)} %bitcast.45, pred[]{:T(512)} %bitcast.46, pred[]{:T(512)} %bitcast.47, pred[]{:T(512)} %bitcast.49, pred[]{:T(512)} %bitcast.48), kind=kLoop, calls=%fused_computation.37 | loop fusion | flops 6144 | bytes 518 | tf_op jit(solution)/shard_map/convert_element_type | solution.py:309
  52.7 3.5 %collective-permute-start.3 = (bf16[8,3,32,16]{2,3,1,0:T(8,128)(2,1)S(1)}, bf16[8,3,32,16]{2,3,1,0:T(8,128)(2,1)S(1)}, u32[]{:S(2)}, u32[]{:S(2)}) collective-permute-start(bf16[8,3,32,16]{2,3,1,0:T(8,128)(2,1)S(1)} %get-tuple-element.9), channel_id=1, source_target_pairs={{0,2},{2,4},{4,6},{1,3},{3,5},{5,7},{8,10},{10,12},{12,14},{9,11},... | collective-permute-start | bytes 73736 | tf_op jit(solution)/shard_map/ppermute | solution.py:28
  56.2 1.3 collective-permute-start.4
  57.5 4.0 %fusion.9 = bf16[256]{0:T(256)(128)(2,1)S(1)} fusion(pred[]{:T(512)} %bitcast.35, pred[]{:T(512)} %bitcast.36, pred[]{:T(512)} %bitcast.37, pred[]{:T(512)} %bitcast.38, pred[]{:T(512)} %bitcast.40, pred[]{:T(512)} %bitcast.39), kind=kLoop, calls=%fused_computation.36 | loop fusion | flops 6144 | bytes 518 | tf_op jit(solution)/shard_map/convert_element_type | solution.py:309
  63.7 1.9 %copy.56 = bf16[8,38,3,16]{1,3,2,0:T(8,128)(2,1)} copy(bf16[8,38,3,16]{2,3,1,0:T(8,128)(2,1)S(1)} %get-tuple-element.7) | data formatting | bytes 58368 | tf_op jit(solution)/shard_map/slice | solution.py:29
  65.5 1.2 copy.57
  66.8 4.9 %collective-permute-start.6 = (bf16[8,38,3,16]{1,3,2,0:T(8,128)(2,1)S(1)}, bf16[8,38,3,16]{1,3,2,0:T(8,128)(2,1)}, u32[]{:S(2)}, u32[]{:S(2)}) collective-permute-start(bf16[8,38,3,16]{1,3,2,0:T(8,128)(2,1)S(1)} %copy.57), channel_id=1, source_target_pairs={{1,0},{3,2},{5,4},{7,6},{9,8},{11,10},{13,12},{15,14},{17,16},{19,... | collective-permute-start | bytes 87560 | tf_op jit(solution)/shard_map/ppermute | solution.py:31
  71.7 1.3 collective-permute-start.5
  73.0 4.0 %fusion.8 = bf16[256]{0:T(256)(128)(2,1)S(1)} fusion(pred[]{:T(512)} %bitcast.26, pred[]{:T(512)} %bitcast.27, pred[]{:T(512)} %bitcast.28, pred[]{:T(512)} %bitcast.29, pred[]{:T(512)} %bitcast.31, pred[]{:T(512)} %bitcast.30), kind=kLoop, calls=%fused_computation.35 | loop fusion | flops 6144 | bytes 518 | tf_op jit(solution)/shard_map/convert_element_type | solution.py:309
  77.0 1.2 copy.58
  78.2 2.1 %copy.59 = bf16[8,38,3,16]{2,3,1,0:T(8,128)(2,1)S(1)} copy(bf16[8,38,3,16]{1,3,2,0:T(8,128)(2,1)} %collective-permute-done.6) | data formatting | bytes 58368 | tf_op jit(solution)/shard_map/ppermute | solution.py:31
  80.3 2.1 %maximum_bitcast_fusion = bf16[38,16,8,38]{3,1,0,2:T(8,128)(2,1)S(1)} fusion(bf16[8,38,3,16]{2,3,1,0:T(8,128)(2,1)S(1)} %copy.59, bf16[8,3,32,16]{2,3,1,0:T(8,128)(2,1)} %copy-done.4, bf16[8,32,32,16]{2,3,1,0:T(8,128)(2,1)S(1)} %constant_dynamic-update-slice_fusion, bf16[8,3,32,16]{2,3,1,0:T(8,128)(2,1)} %copy-done.3, bf16[8,38,3,16]{2,3,1,0:T(8,128)(2,1)S(1)} %copy.58), kind=kLoop, calls=%fused_computation.1 | loop fusion | flops 1848320 | bytes 739328 | tf_op jit(solution)/shard_map/transpose | solution.py:298
  83.2 0.9 reshape.162
  85.5 1.6 copy-done.2
  87.1 88.6 %block.1 = bf16[2,32,32,384]{3,2,1,0:T(8,128)(2,1)} custom-call(s32[20]{0:T(128)} %stack.168.ints, f32[12,4]{1,0:T(8,128)} %stack.193.coefs, bf16[9,608,256]{2,1,0:T(8,128)(2,1)} %copy-done.2, bf16[432,384]{1,0:T(8,128)(2,1)} %bitcast.87, f32[256,1]{1,0:T(8,128)} %and_convert_fusion.keep_ref, f32[1,384]{1,0:T(1,128)} %mul.119.g1_ref, f32[1,384]{1,0:T(1,128)} %mul.121.g2_ref, ...), custom_call_target="tpu_custom_call" | custom-call | tf_op jit(solution)/shard_map/block/pallas_call | solution.py:348
  (47 shorter events, 6.9 us)
Async XLA Ops:
  0.0 52.5 %collective-permute-start.1 = (bf16[2,32,32,16]{2,3,1,0:T(8,128)(2,1)}, bf16[2,32,32,16]{2,3,1,0:T(8,128)(2,1)S(1)}, u32[]{:S(2)}, u32[]{:S(2)}) collective-permute-start(bf16[2,32,32,16]{2,3,1,0:T(8,128)(2,1)} %param.7), channel_id=1, source_target_pairs={{0,16},{8,24},{16,32},{24,40},{32,48},{40,56},{48,64},{56,72},{64,... | collective-permute-start | bytes 196616 | tf_op jit(solution)/shard_map/ppermute | solution.py:20
  5.7 46.8 %collective-permute-start = (bf16[2,32,32,16]{2,3,1,0:T(8,128)(2,1)}, bf16[2,32,32,16]{2,3,1,0:T(8,128)(2,1)S(1)}, u32[]{:S(2)}, u32[]{:S(2)}) collective-permute-start(bf16[2,32,32,16]{2,3,1,0:T(8,128)(2,1)} %param.7), channel_id=1, source_target_pairs={{0,24},{8,32},{16,40},{24,48},{32,56},{40,64},{48,72},{56,80},{64,... | collective-permute-start | bytes 196616 | tf_op jit(solution)/shard_map/ppermute | solution.py:20
  9.3 43.3 %collective-permute-start.2 = (bf16[2,32,32,16]{2,3,1,0:T(8,128)(2,1)}, bf16[2,32,32,16]{2,3,1,0:T(8,128)(2,1)S(1)}, u32[]{:S(2)}, u32[]{:S(2)}) collective-permute-start(bf16[2,32,32,16]{2,3,1,0:T(8,128)(2,1)} %param.7), channel_id=1, source_target_pairs={{0,8},{8,16},{16,24},{24,32},{32,40},{40,48},{48,56},{56,64},{64,7... | collective-permute-start | bytes 196616 | tf_op jit(solution)/shard_map/ppermute | solution.py:20
  26.8 3.3 %copy-start = (bf16[3,3,3,384,384]{4,3,2,1,0:T(8,128)(2,1)S(1)}, bf16[3,3,3,384,384]{4,3,2,1,0:T(8,128)(2,1)}, u32[]{:S(2)}) copy-start(bf16[3,3,3,384,384]{4,3,2,1,0:T(8,128)(2,1)} %w_ref.2) | copy-start | bytes 23887876
  30.0 9.2 %copy-start.1 = (bf16[3,3,3,384,384]{4,3,2,1,0:T(8,128)(2,1)S(1)}, bf16[3,3,3,384,384]{4,3,2,1,0:T(8,128)(2,1)}, u32[]{:S(2)}) copy-start(bf16[3,3,3,384,384]{4,3,2,1,0:T(8,128)(2,1)} %w_ref.3) | copy-start | bytes 23887876
  39.3 13.3 %copy-start.5 = (bf16[2,32,32,16]{2,3,1,0:T(8,128)(2,1)S(1)}, bf16[2,32,32,16]{2,3,1,0:T(8,128)(2,1)}, u32[]{:S(2)}) copy-start(bf16[2,32,32,16]{2,3,1,0:T(8,128)(2,1)} %param.7) | copy-start | bytes 196612
  52.7 8.9 %collective-permute-start.3 = (bf16[8,3,32,16]{2,3,1,0:T(8,128)(2,1)S(1)}, bf16[8,3,32,16]{2,3,1,0:T(8,128)(2,1)S(1)}, u32[]{:S(2)}, u32[]{:S(2)}) collective-permute-start(bf16[8,3,32,16]{2,3,1,0:T(8,128)(2,1)S(1)} %get-tuple-element.9), channel_id=1, source_target_pairs={{0,2},{2,4},{4,6},{1,3},{3,5},{5,7},{8,10},{10,12},{12,14},{9,11},... | collective-permute-start | bytes 73736 | tf_op jit(solution)/shard_map/ppermute | solution.py:28
  56.2 5.5 %collective-permute-start.4 = (bf16[8,3,32,16]{2,3,1,0:T(8,128)(2,1)S(1)}, bf16[8,3,32,16]{2,3,1,0:T(8,128)(2,1)S(1)}, u32[]{:S(2)}, u32[]{:S(2)}) collective-permute-start(bf16[8,3,32,16]{2,3,1,0:T(8,128)(2,1)S(1)} %get-tuple-element.10), channel_id=1, source_target_pairs={{2,0},{4,2},{6,4},{3,1},{5,3},{7,5},{10,8},{12,10},{14,12},{11,9},... | collective-permute-start | bytes 73736 | tf_op jit(solution)/shard_map/ppermute | solution.py:31
  61.5 0.6 copy-start.3
  62.2 0.6 copy-start.4
  66.8 11.4 %collective-permute-start.6 = (bf16[8,38,3,16]{1,3,2,0:T(8,128)(2,1)S(1)}, bf16[8,38,3,16]{1,3,2,0:T(8,128)(2,1)}, u32[]{:S(2)}, u32[]{:S(2)}) collective-permute-start(bf16[8,38,3,16]{1,3,2,0:T(8,128)(2,1)S(1)} %copy.57), channel_id=1, source_target_pairs={{1,0},{3,2},{5,4},{7,6},{9,8},{11,10},{13,12},{15,14},{17,16},{19,... | collective-permute-start | bytes 87560 | tf_op jit(solution)/shard_map/ppermute | solution.py:31
  71.7 5.3 %collective-permute-start.5 = (bf16[8,38,3,16]{1,3,2,0:T(8,128)(2,1)}, bf16[8,38,3,16]{1,3,2,0:T(8,128)(2,1)S(1)}, u32[]{:S(2)}, u32[]{:S(2)}) collective-permute-start(bf16[8,38,3,16]{1,3,2,0:T(8,128)(2,1)} %copy.56), channel_id=1, source_target_pairs={{0,1},{2,3},{4,5},{6,7},{8,9},{10,11},{12,13},{14,15},{16,17},{18,... | collective-permute-start | bytes 87560 | tf_op jit(solution)/shard_map/ppermute | solution.py:28
  85.5 1.6 copy-start.2
where the time goes:
time: 177 us; the launch traced here: 176 us
  Pallas kernels  107 us (60%)
  starting transfers between devices  22.9 us (13%)
  local copies, waits for them, and re-layouts  21.6 us (12%)
  other arithmetic  19.8 us (11%)
  between operations  4.27 us (2%)
    pallas_call x1, Pallas kernels, body(): pl.pallas_call(main_kernel, in_specs=[smem, smem, vmem, vmem, vmem, vmem,...  88.6 us
    pallas_call x2, Pallas kernels, transformed_weights(): pl.pallas_call(weights_kernel, grid=(3, C // chunk), in_specs=[pl.BlockSp...  18.4 us
    convert_element_type x3, other arithmetic, body(): mask = (distance >= lag)[frame_of].astype(BF)  12 us
    ppermute x3, starting transfers between devices, passed_along(): return lax.ppermute(block, axis, route)  11.9 us
    unnamed x16, local copies, waits for them, and re-layouts  6.45 us
    ppermute x2, starting transfers between devices, padded(): lax.ppermute(lax.slice_in_dim(block, 0, width, axis=dim), axis, backward)  6.2 us
    ppermute x2, starting transfers between devices, padded(): lax.ppermute(lax.slice_in_dim(block, block.shape[dim] - width, None, axis...  4.83 us
  transfers between devices with their start and end apart: 7, of which 1 were waited for; matrix products, arithmetic and copies ran while one was open for 14% of the time, Pallas kernels for 10%

commit v1 on v0

v1 whole, which is shorter than its diff:
```python
import functools

import jax
import jax.numpy as jnp
from jax import lax
from jax.experimental import pallas as pl
from jax.experimental.pallas import tpu as pltpu
from jax.sharding import PartitionSpec as P

C = 384
K3 = 3 * C
MIB = 2**20
BF = jnp.bfloat16
F32 = jnp.float32


MESH = pl.DeviceIdType.MESH
ROWS = 32
COLS = 32
HALO = 3
BAND = 16 + 2 * HALO
SOURCES = 4
WEIGHT_STEPS = 9
LAST = 2 * WEIGHT_STEPS - 1
PARTNERS = [(k, d) for k in range(SOURCES) for d in (0, 1, -1) if (k, d) != (0, 0)]
SENT = {0: (0, 16), 1: (16 - HALO, HALO), -1: (0, HALO)}
LANDS = {0: HALO, 1: 0, -1: HALO + 16}
SETS = 14


def weight_block(w_ref, u_ref):
    step = 16

    @pl.loop(0, w_ref.shape[3] // step)
    def _(block):
        part = pl.ds(pl.multiple_of(block * step, step), step)
        w = [[w_ref[t, y, 0, part, :].astype(F32) for y in range(3)] for t in range(3)]
        edge = [w[0][y] + w[2][y] for y in range(3)]
        times = [
            w[0],
            [(edge[y] + w[1][y]) * 0.5 for y in range(3)],
            [(edge[y] - w[1][y]) * 0.5 for y in range(3)],
            w[2],
            w[1],
        ]
        for t, g in enumerate(times):
            outer = g[0] + g[2]
            u_ref[2 * t, 0, part, :] = ((outer + g[1]) * 0.5).astype(BF)
            u_ref[2 * t + 1, 0, part, :] = ((outer - g[1]) * 0.5).astype(BF)
        for n, t in enumerate((1, 2)):
            u_ref[10 + 2 * n, 0, part, :] = times[t][0].astype(BF)
            u_ref[11 + 2 * n, 0, part, :] = times[t][2].astype(BF)


def gather_kernel(
    own_ref, w1_ref, w2_ref, all_ref, u1_ref, u2_ref, send_sem, recv_sem, local_sem, pair_sem
):
    step = pl.program_id(0)
    tm = lax.axis_index("tm")
    sy = lax.axis_index("sy")
    sx = lax.axis_index("sx")
    tms = lax.axis_size("tm")
    sys = lax.axis_size("sy")

    def place(k, d):
        return (lax.rem(tm + k + tms, tms), lax.rem(sy + d + sys, sys), sx)

    def copy(n):
        k, d = PARTNERS[n]
        first, count = SENT[d]
        return pltpu.make_async_remote_copy(
            src_ref=own_ref.at[pl.ds(first, count)],
            dst_ref=all_ref.at[SOURCES - 1 - k, sx, pl.ds(LANDS[d], count)],
            send_sem=send_sem.at[n],
            recv_sem=recv_sem.at[n],
            device_id=place(k, d),
            device_id_type=MESH,
        )

    def local():
        return pltpu.make_async_copy(
            own_ref, all_ref.at[SOURCES - 1, sx, pl.ds(HALO, 16)], local_sem
        )

    def across():
        return pltpu.make_async_remote_copy(
            src_ref=all_ref.at[:, sx],
            dst_ref=all_ref.at[:, sx],
            send_sem=pair_sem.at[0],
            recv_sem=pair_sem.at[1],
            device_id=(tm, sy, 1 - sx),
            device_id_type=MESH,
        )

    @pl.when(step == 0)
    def _():
        barrier = pltpu.get_barrier_semaphore()
        for k, d in PARTNERS:
            pl.semaphore_signal(barrier, inc=1, device_id=place(-k, -d), device_id_type=MESH)
        pl.semaphore_signal(barrier, inc=1, device_id=(tm, sy, 1 - sx), device_id_type=MESH)
        local().start()
        pl.semaphore_wait(barrier, len(PARTNERS) + 1)
        for n in range(len(PARTNERS)):
            copy(n).start()

    @pl.when(step < WEIGHT_STEPS)
    def _():
        weight_block(w1_ref, u1_ref)

    @pl.when(step >= WEIGHT_STEPS)
    def _():
        weight_block(w2_ref, u2_ref)

    @pl.when(step == WEIGHT_STEPS)
    def _():
        local().wait()
        for n in range(len(PARTNERS)):
            copy(n).wait()
        across().start()

    @pl.when(step == LAST)
    def _():
        across().wait()


def gathered(own, first_kernel, second_kernel):
    chunk = C // 3
    hbm = pl.BlockSpec(memory_space=pl.ANY)

    def spec(shape, lead, shift):
        def index(step):
            block = jnp.clip(step - shift, 0, WEIGHT_STEPS - 1)
            return (0,) * lead + (block // 3, block % 3, 0)

        return pl.BlockSpec(shape, index)

    copies = len(PARTNERS)
    sets = jax.ShapeDtypeStruct((SETS, 3, C, C), BF)
    return pl.pallas_call(
        gather_kernel,
        grid=(LAST + 1,),
        in_specs=[
            hbm,
            spec((3, 3, 1, chunk, C), 2, 0),
            spec((3, 3, 1, chunk, C), 2, WEIGHT_STEPS),
        ],
        out_specs=[
            hbm,
            spec((SETS, 1, chunk, C), 1, 0),
            spec((SETS, 1, chunk, C), 1, WEIGHT_STEPS),
        ],
        out_shape=[jax.ShapeDtypeStruct((SOURCES, 2, BAND, 16, 128), BF), sets, sets],
        scratch_shapes=[
            pltpu.SemaphoreType.DMA((copies,)),
            pltpu.SemaphoreType.DMA((copies,)),
            pltpu.SemaphoreType.DMA,
            pltpu.SemaphoreType.DMA((2,)),
        ],
        compiler_params=pltpu.CompilerParams(
            vmem_limit_bytes=62 * MIB, collective_id=0, has_side_effects=True
        ),
        cost_estimate=pl.CostEstimate(
            flops=60 * 9 * C * C, bytes_accessed=2 * 41 * 3 * C * C * 2, transcendentals=0
        ),
        name="gather",
    )(own, first_kernel, second_kernel)


WIDE = 40
LEAD = 9
CELLS = 256
R1 = ROWS + 4
R2 = ROWS + 2
I1 = R2 // 2
I2 = ROWS // 2
M1 = I1 * COLS + 32
M2 = I2 * COLS
HALF = 24
ENTRY_ROWS = 4


def norm_act(values, gain, keep):
    mean = jnp.mean(values * values, axis=-1, keepdims=True)
    half = values * (lax.rsqrt(mean + 1e-6) * keep) * gain
    return half * jnp.tanh(half) + half


def splat(value, shape):
    one = jnp.full((16, 128), value, F32).astype(BF)
    return jnp.tile(one, (shape[0] // 16, shape[1] // 128))


def clip_scalars(lengths, first, count):
    found = [jnp.int32(0)] * count
    start = jnp.int32(0)
    for k in range(lengths.shape[0]):
        for n in range(count):
            t = first + n
            found[n] = jnp.where(start <= t, t - start, found[n])
        start = start + lengths[k]
    return found


def spread_latents(all_ref, q_ref, distance, sx, top, bottom):
    depth = SOURCES * 2 * 128
    index = lax.broadcasted_iota(jnp.int32, (depth, 1), 0)
    source = index // 256
    side = (index // 128) % 2
    half = (index // 64) % 2
    frame = (index // 32) % 2
    x = index % 32
    column = jnp.where(side == sx, x, jnp.where(sx == 0, x + COLS, x - COLS))
    wanted = (column >= -HALO) & (column < COLS + HALO)
    target = (2 * source + frame) * WIDE + column + LEAD + 1
    lane = lax.broadcasted_iota(jnp.int32, (depth, 384), 1)
    spread = []
    for h in range(2):
        to = jnp.where(wanted & (half == h), target, -1)
        pick = jnp.where(lane == to, 1.0, 0.0).astype(BF)
        bands = (0, 16 + HALO) if h else (HALO, BAND)
        rows = (bands[1] - bands[0]) * 16
        lhs = jnp.concatenate(
            [
                all_ref[t, s, bands[0] : bands[1]].reshape(rows, 128)
                for t in range(SOURCES)
                for s in range(2)
            ],
            axis=1,
        )
        spread.append(jnp.dot(lhs, pick, preferred_element_type=F32))
    lower, upper = spread
    edge = HALO * 16
    pt = jnp.concatenate(
        [
            upper[:edge] * top.astype(F32),
            lower[: 16 * 16],
            upper[edge:],
            lower[16 * 16 :] * bottom.astype(F32),
        ],
        axis=0,
    )
    lane = lax.broadcasted_iota(jnp.int32, (1, CELLS), 1)
    frame_of = (lane - (LEAD - 4)) // WIDE
    for lag in range(3):
        keep = jnp.zeros((1, CELLS), F32)
        for f in range(6):
            seen = (distance[f] >= lag).astype(F32)
            keep = jnp.where(frame_of == f, seen, keep)
        for dx in range(3):
            first = (2 - lag) * WIDE + dx
            moved = pltpu.roll(pt, 384 - first, axis=1) if first else pt
            q_ref[3 * lag + dx] = (moved[:, :CELLS] * keep).astype(BF)


def main_kernel(
    lengths, all_ref, we_ref, g1_ref, g2_ref, w1_hbm, w2_hbm, u1_hbm, u2_hbm,
    out_ref,
    q_ref, f_ref, h_ref, s_ref, e_ref, x_ref, m_ref, acc_ref, w_ref, a_ref, b_ref, hn_ref,
    keep_ref, table, coefs, sem,
):
    tm = lax.axis_index("tm")
    sy = lax.axis_index("sy")
    sx = lax.axis_index("sx")
    top = (sy > 0).astype(jnp.int32)
    bottom = (sy < lax.axis_size("sy") - 1).astype(jnp.int32)
    halo_place = jnp.where(sx == 0, COLS, -1) + LEAD - 1
    halo_slot = jnp.where(sx == 0, 8 + COLS, 7)
    zero_slot = jnp.where(sx == 0, 7, 8 + COLS)
    distance = clip_scalars(lengths, 2 * tm - 4, 6)

    for n, pair in enumerate((0, 1, 1)):
        da = distance[2 + 2 * pair]
        whole = distance[3 + 2 * pair] >= 1
        k0 = (da >= 2).astype(F32)
        k1 = (da >= 1).astype(F32)
        s = whole.astype(F32)
        lines = [
            (k0, -s, 1.0, 0.0),
            (k1, s, 1.0, s),
            (1.0, -s * k1, 1.0, -s),
            (s * k1, -1.0, 0.0, -1.0),
        ]
        for tau, line in enumerate(lines):
            for k, value in enumerate(line):
                coefs[4 * n + tau, k] = jnp.float32(value)
        table[4 * n] = 0
        table[4 * n + 1] = jnp.where(whole, 1, 4)
        table[4 * n + 2] = jnp.where(whole, 2, 3)
        table[4 * n + 3] = 3

    def pieces(step, slot, w_hbm, u_hbm):
        which = table[step]
        mixed = pltpu.make_async_copy(
            u_hbm.at[pl.ds(2 * which, 2)], w_ref.at[slot, pl.ds(1, 2)], sem.at[slot, 0]
        )
        tap = jnp.where(which == 0, 0, jnp.where(which == 3, 2, 1))
        time_set = 10 + 2 * jnp.where(which == 2, 1, 0)
        plain = [
            pltpu.make_async_copy(w_hbm.at[tap, 2 * n], w_ref.at[slot, 3 * n], sem.at[slot, 1 + n])
            for n in range(2)
        ]
        made = [
            pltpu.make_async_copy(
                u_hbm.at[time_set + n], w_ref.at[slot, 3 * n], sem.at[slot, 1 + n]
            )
            for n in range(2)
        ]
        return which, mixed, plain, made

    def fetch(step, slot, w_hbm=w1_hbm, u_hbm=u1_hbm):
        which, mixed, plain, made = pieces(step, slot, w_hbm, u_hbm)
        mixed.start()
        time_mixed = (which == 1) | (which == 2)

        @pl.when(time_mixed)
        def _():
            for one in made:
                one.start()

        @pl.when(jnp.logical_not(time_mixed))
        def _():
            for one in plain:
                one.start()

    def arrive(step, slot, w_hbm=w1_hbm, u_hbm=u1_hbm):
        _, mixed, _, made = pieces(step, slot, w_hbm, u_hbm)
        mixed.wait()
        for one in made:
            one.wait()

    fetch(0, 0)
    spread_latents(all_ref, q_ref, distance, sx, top, bottom)
    place = lax.broadcasted_iota(jnp.int32, (CELLS, 128), 0)
    column = place - LEAD - ((place - (LEAD - 4)) // WIDE) * WIDE
    low = jnp.where(sx == 0, 0, -2)
    high = jnp.where(sx == 0, COLS + 2, COLS)
    keep_ref[...] = jnp.where((column >= low) & (column < high), 1.0, 0.0)
    first_gain = g1_ref[...][None, :] * 0.5
    second_gain = g2_ref[...][None, :] * 0.5

    h_ref[...] = jnp.zeros_like(h_ref)

    @pl.loop(0, R1 // ENTRY_ROWS)
    def _(block):
        cols = []
        for n in range(ENTRY_ROWS):
            first = pl.multiple_of((block * ENTRY_ROWS + n) * 16, 16)
            cols.append(
                jnp.concatenate(
                    [
                        q_ref[3 * lag + dx, pl.ds(first + 16 * dy, 16), :]
                        for lag in (2, 1, 0)
                        for dy in range(3)
                        for dx in range(3)
                    ],
                    axis=0,
                )
            )
        patches = jnp.concatenate(cols, axis=1)
        entry = lax.dot_general(
            patches, we_ref[...], (((0,), (0,)), ((), ())), preferred_element_type=F32
        ).astype(BF)
        for n in range(ENTRY_ROWS):
            row = block * ENTRY_ROWS + n
            inside = jnp.where(row < 2, top, jnp.where(row >= R1 - 2, bottom, 1)).astype(F32)
            value = entry[n * CELLS : (n + 1) * CELLS].astype(F32)
            b_ref[n] = value
            a_ref[n] = norm_act(value, first_gain, keep_ref[:, :1] * inside)
        for n in range(ENTRY_ROWS):
            row = block * ENTRY_ROWS + n
            for f in range(2):
                e_ref[f, row] = b_ref[n, pl.ds((4 + f) * WIDE + LEAD, COLS), :].astype(BF)
            for f in range(6):
                for dx in range(3):
                    lanes = slice(dx * C, (dx + 1) * C)
                    place = f * WIDE + LEAD - 1 + dx
                    f_ref[f, row, :, lanes] = a_ref[n, pl.ds(place, COLS), :].astype(BF)
                    h_ref[f, n % 2, pl.ds(row // 2, 1), lanes] = a_ref[
                        n, pl.ds(f * WIDE + halo_place + dx, 1), :
                    ]

    def products(step, slot, rows):
        for k in range(4):
            m_ref[k, :rows, :] = jnp.dot(
                x_ref[k, :rows, :], w_ref[slot, k], preferred_element_type=F32
            )
        first = coefs[step, 2]
        second = coefs[step, 3]

        @pl.loop(0, rows // COLS)
        def _(i):
            part = pl.ds(pl.multiple_of(i * COLS, COLS), COLS)
            terms = [m_ref[k, part, :] for k in range(4)]
            even = terms[0] + terms[1] + terms[2]
            odd = terms[1] - terms[2] - terms[3]
            for parity, value in enumerate((even, odd)):
                acc_ref[0, parity, part, :] += first * value
                acc_ref[1, parity, part, :] += second * value

    def row_transform(d):
        return d[0] - d[2], d[1] + d[2], d[2] - d[1], d[1] - d[3]

    def frames_of(tau, base):
        one = jnp.where(tau == 0, 0, jnp.where(tau == 2, 2, 1)) + base
        other = jnp.where(tau == 2, 1, jnp.where(tau == 3, 3, 2)) + base
        return one, other

    def build(source, rows, step, one, other):
        shape = (COLS, K3)
        c_one = splat(coefs[step, 0], shape)
        c_other = splat(coefs[step, 1], shape)

        @pl.loop(0, rows)
        def _(i):
            d = [
                c_one * source[one, 2 * i + k] + c_other * source[other, 2 * i + k]
                for k in range(4)
            ]
            for k, value in enumerate(row_transform(d)):
                x_ref[k, pl.ds(pl.multiple_of(i * COLS, COLS), COLS), :] = value

    @pl.loop(0, 8)
    def _(step):
        slot = lax.rem(step, 2)
        tau = lax.rem(step, 4)
        pair = step // 4
        arrive(step, slot)

        @pl.when(step < 7)
        def _():
            fetch(step + 1, 1 - slot)

        @pl.when(step == 7)
        def _():
            fetch(step + 1, 1 - slot, w2_hbm, u2_hbm)

        one, other = frames_of(tau, 2 * pair)
        build(f_ref, I1, step, one, other)
        d = []
        for k in range(4):
            part = pl.ds(k // 2, HALF)
            d.append(
                coefs[step, 0] * h_ref[one, k % 2, part, :]
                + coefs[step, 1] * h_ref[other, k % 2, part, :]
            )
        for k, value in enumerate(row_transform(d)):
            both = jnp.concatenate([value, jnp.zeros((32 - HALF, K3), F32)], axis=0)
            x_ref[k, I1 * COLS :, :] = both.astype(BF)

        @pl.when(tau == 0)
        def _():
            acc_ref[...] = jnp.zeros_like(acc_ref)

        products(step, slot, M1)

        @pl.when(tau == 3)
        def _():
            for member in range(2):
                frame = 2 * pair + member
                for parity in range(2):
                    hn_ref[parity] = norm_act(
                        acc_ref[member, parity, I1 * COLS :, :], second_gain, 1.0
                    )

                @pl.loop(0, I1)
                def _(i):
                    for parity in range(2):
                        row = 2 * i + parity
                        inside = jnp.where(
                            row == 0, top, jnp.where(row == R2 - 1, bottom, 1)
                        ).astype(F32)
                        part = pl.ds(pl.multiple_of(i * COLS, COLS), COLS)
                        value = norm_act(acc_ref[member, parity, part, :], second_gain, inside)
                        a_ref[parity, pl.ds(8, COLS), :] = value
                        a_ref[parity, pl.ds(halo_slot, 1), :] = (
                            hn_ref[parity, pl.ds(i, 1), :] * inside
                        )
                        a_ref[parity, pl.ds(zero_slot, 1), :] = jnp.zeros((1, C), F32)
                        for dx in range(3):
                            s_ref[frame, row, :, dx * C : (dx + 1) * C] = a_ref[
                                parity, pl.ds(7 + dx, COLS), :
                            ].astype(BF)

    acc_ref[...] = jnp.zeros_like(acc_ref)

    @pl.loop(8, 12)
    def _(step):
        slot = lax.rem(step, 2)
        tau = lax.rem(step, 4)
        arrive(step, slot, w2_hbm, u2_hbm)

        @pl.when(step < 11)
        def _():
            fetch(step + 1, 1 - slot, w2_hbm, u2_hbm)

        one, other = frames_of(tau, 0)
        build(s_ref, I2, step, one, other)
        products(step, slot, M2)

    for member in range(2):

        @pl.loop(0, I2)
        def _(i):
            for parity in range(2):
                row = 2 * i + parity
                part = pl.ds(pl.multiple_of(i * COLS, COLS), COLS)
                out_ref[member, row] = (
                    acc_ref[member, parity, part, :] + e_ref[member, row + 2].astype(F32)
                ).astype(BF)


def block_call(*operands):
    vmem = pl.BlockSpec(memory_space=pltpu.VMEM)
    smem = pl.BlockSpec(memory_space=pltpu.SMEM)
    hbm = pl.BlockSpec(memory_space=pl.ANY)
    return pl.pallas_call(
        main_kernel,
        in_specs=[smem, vmem, vmem, vmem, vmem, hbm, hbm, hbm, hbm],
        out_specs=vmem,
        out_shape=jax.ShapeDtypeStruct((2, ROWS, COLS, C), BF),
        scratch_shapes=[
            pltpu.VMEM((9, 38 * 16, CELLS), BF),
            pltpu.VMEM((6, R1, COLS, K3), BF),
            pltpu.VMEM((6, 2, HALF + 8, K3), F32),
            pltpu.VMEM((4, R2, COLS, K3), BF),
            pltpu.VMEM((2, R1, COLS, C), BF),
            pltpu.VMEM((4, M1, K3), BF),
            pltpu.VMEM((4, M1, C), F32),
            pltpu.VMEM((2, 2, M1, C), F32),
            pltpu.VMEM((2, 4, K3, C), BF),
            pltpu.VMEM((ENTRY_ROWS, CELLS, C), F32),
            pltpu.VMEM((ENTRY_ROWS, CELLS, C), F32),
            pltpu.VMEM((2, 32, C), F32),
            pltpu.VMEM((CELLS, 128), F32),
            pltpu.SMEM((12,), jnp.int32),
            pltpu.SMEM((12, 4), F32),
            pltpu.SemaphoreType.DMA((2, 3)),
        ],
        compiler_params=pltpu.CompilerParams(vmem_limit_bytes=62 * MIB),
        name="block",
    )(*operands)


def body(latent, clip_lengths, entry_kernel, first_gain, first_kernel, second_gain, second_kernel):
    own = latent.reshape(2, 2, 16, COLS, 16).transpose(2, 4, 1, 0, 3).reshape(16, 16, 128)
    everything, u1, u2 = gathered(own, first_kernel, second_kernel)
    return block_call(
        clip_lengths,
        everything,
        entry_kernel.reshape(27 * 16, C),
        first_gain,
        second_gain,
        first_kernel.reshape(3, 3, K3, C),
        second_kernel.reshape(3, 3, K3, C),
        u1.reshape(SETS, K3, C),
        u2.reshape(SETS, K3, C),
    )


def solution(mesh):
    return jax.shard_map(
        body,
        mesh=mesh,
        in_specs=(P("tm", "sy", "sx", None), P(), P(), P(), P(), P(), P()),
        out_specs=P("tm", "sy", "sx", None),
        check_vma=False,
    )
```

time: 177 us -> 123 us (0.69)
  starting transfers between devices: 22.9 us -> 0 us
  other arithmetic: 19.8 us -> 0 us
  local copies, waits for them, and re-layouts: 21.6 us -> 2.02 us
  Pallas kernels: 107 us -> 121 us
  between operations: 4.27 us -> 0.01 us
    ppermute x7 -> x0, starting transfers between devices: 22.9 us -> none  [the longest x3 11.9 us: passed_along(): return lax.ppermute(block, axis, route)]
    pallas_call x3 -> x2, Pallas kernels: 107 us -> 121 us  [the longest x1 90.4 us: block_call(): pl.pallas_call(main_kernel, in_specs=[smem, vmem, vmem, vmem, vmem, hbm,...]
    convert_element_type x4 -> x0, other arithmetic: 12.7 us -> none  [the longest x3 12 us: body(): mask = (distance >= lag)[frame_of].astype(BF)]
    unnamed x16 -> x0, local copies, waits for them, and re-layouts: 6.45 us -> none
    slice x5 -> x0, local copies, waits for them, and re-layouts: 4.36 us -> none  [the longest x3 2.46 us: padded(): lax.slice_in_dim(block, block.shape[dim] - width, None, axis=dim)]
    ppermute x2 -> x0, local copies, waits for them, and re-layouts: 3.27 us -> none  [the longest x1 2.08 us: padded(): lax.ppermute(lax.slice_in_dim(block, 0, width, axis=dim), axis, backward)]
    transpose x1 -> x0, other arithmetic: 2.08 us -> none  [body(): across = jnp.transpose(window, (1, 3, 0, 2))]
    another operation x3 -> x0, local copies, waits for them, and re-layouts: 1.91 us -> none  [the longest x1 1.22 us: body(): jnp.stack([jnp.stack([jnp.asarray(v, F32) for v in line]) for line in coe...]
  transfers between devices with their start and end apart: 7 -> 0, of which waited for: 1 -> 0; matrix products, arithmetic and copies ran while one was open for 14% -> 0% of each run, Pallas kernels for 10% -> 0%
where the time goes in v1:
time: 123 us
  Pallas kernels  121 us (98%)
  local copies, waits for them, and re-layouts  2.02 us (2%)
    pallas_call x1, Pallas kernels, block_call(): pl.pallas_call(main_kernel, in_specs=[smem, vmem, vmem, vmem, vmem, hbm,...  90.4 us
    pallas_call x1, Pallas kernels, gathered(): pl.pallas_call(gather_kernel, grid=(LAST + 1,), in_specs=[hbm, spec((3, 3...  30.4 us

profile of v1, /device:TPU:1, one launch (start us, length us, event | category | flops | bytes accessed | tf_op | source)
XLA Modules:
  0.0 122.8 jit_solution(15707140370321659070)
XLA Ops:
  0.0 1.2 copy.10
  1.2 0.8 reshape.22.own_ref
  2.0 30.4 %gather.1 = (bf16[4,2,22,16,128]{4,3,2,1,0:T(8,128)(2,1)}, bf16[14,3,384,384]{3,2,1,0:T(8,128)(2,1)}, bf16[14,3,384,384]{3,2,1,0:T(8,128)(2,1)}) custom-call(bf16[16,16,128]{2,1,0:T(8,128)(2,1)} %reshape.22.own_ref, bf16[3,3,3,384,384]{4,3,2,1,0:T(8,128)(2,1)} %w1_ref.1, bf16[3,3,3,384,384]{4,3,2,1,0:T(8,128)(2,1)} %w2_ref.1), custom_call_target="tpu_custom_call" | custom-call | flops 79626240 | bytes 72548352 | tf_op jit(solution)/shard_map/gather/pallas_call | solution.py:139
  32.5 90.4 %block.1 = bf16[2,32,32,384]{3,2,1,0:T(8,128)(2,1)} custom-call(s32[9]{0:T(128)} %lengths.1, bf16[4,2,22,16,128]{4,3,2,1,0:T(8,128)(2,1)} %get-tuple-element.8.all_ref, bf16[432,384]{1,0:T(8,128)(2,1)} %bitcast.14, f32[384]{0:T(512)} %g1_ref.1, f32[384]{0:T(512)} %g2_ref.1, bf16[3,3,1152,384]{3,2,1,0:T(8,128)(2,1)} %bitcast.9, ...), custom_call_target="tpu_custom_call" | custom-call | tf_op jit(solution)/shard_map/block/pallas_call | solution.py:516

commit v2 on v1

v2 whole, which is shorter than its diff:
```python
import functools

import jax
import jax.numpy as jnp
from jax import lax
from jax.experimental import pallas as pl
from jax.experimental.pallas import tpu as pltpu
from jax.sharding import PartitionSpec as P

C = 384
K3 = 3 * C
MIB = 2**20
BF = jnp.bfloat16
F32 = jnp.float32


MESH = pl.DeviceIdType.MESH
ROWS = 32
COLS = 32
HALO = 3
BAND = 16 + 2 * HALO
SOURCES = 4
WEIGHT_STEPS = 9
LAST = 2 * WEIGHT_STEPS - 1
PARTNERS = [(k, d) for k in range(SOURCES) for d in (0, 1, -1) if (k, d) != (0, 0)]
SENT = {0: (0, 16), 1: (16 - HALO, HALO), -1: (0, HALO)}
LANDS = {0: HALO, 1: 0, -1: HALO + 16}
SETS = 14
ENTERED = 2


def weight_block(w_ref, u_ref):
    step = 16

    @pl.loop(0, w_ref.shape[3] // step)
    def _(block):
        part = pl.ds(pl.multiple_of(block * step, step), step)
        w = [[w_ref[t, y, 0, part, :].astype(F32) for y in range(3)] for t in range(3)]
        edge = [w[0][y] + w[2][y] for y in range(3)]
        times = [
            w[0],
            [(edge[y] + w[1][y]) * 0.5 for y in range(3)],
            [(edge[y] - w[1][y]) * 0.5 for y in range(3)],
            w[2],
            w[1],
        ]
        for t, g in enumerate(times):
            outer = g[0] + g[2]
            u_ref[2 * t, 0, part, :] = ((outer + g[1]) * 0.5).astype(BF)
            u_ref[2 * t + 1, 0, part, :] = ((outer - g[1]) * 0.5).astype(BF)
        for n, t in enumerate((1, 2)):
            u_ref[10 + 2 * n, 0, part, :] = times[t][0].astype(BF)
            u_ref[11 + 2 * n, 0, part, :] = times[t][2].astype(BF)


def gather_kernel(
    own_ref, w1_ref, w2_ref, all_ref, u1_ref, u2_ref, send_sem, recv_sem, local_sem, pair_sem
):
    step = pl.program_id(0)
    tm = lax.axis_index("tm")
    sy = lax.axis_index("sy")
    sx = lax.axis_index("sx")
    tms = lax.axis_size("tm")
    sys = lax.axis_size("sy")

    def place(k, d):
        return (lax.rem(tm + k + tms, tms), lax.rem(sy + d + sys, sys), sx)

    def copy(n):
        k, d = PARTNERS[n]
        first, count = SENT[d]
        return pltpu.make_async_remote_copy(
            src_ref=own_ref.at[pl.ds(first, count)],
            dst_ref=all_ref.at[SOURCES - 1 - k, sx, pl.ds(LANDS[d], count)],
            send_sem=send_sem.at[n],
            recv_sem=recv_sem.at[n],
            device_id=place(k, d),
            device_id_type=MESH,
        )

    def local():
        return pltpu.make_async_copy(
            own_ref, all_ref.at[SOURCES - 1, sx, pl.ds(HALO, 16)], local_sem
        )

    def across():
        return pltpu.make_async_remote_copy(
            src_ref=all_ref.at[:, sx],
            dst_ref=all_ref.at[:, sx],
            send_sem=pair_sem.at[0],
            recv_sem=pair_sem.at[1],
            device_id=(tm, sy, 1 - sx),
            device_id_type=MESH,
        )

    @pl.when(step == 0)
    def _():
        barrier = pltpu.get_barrier_semaphore()
        for k, d in PARTNERS:
            pl.semaphore_signal(barrier, inc=1, device_id=place(-k, -d), device_id_type=MESH)
        pl.semaphore_signal(barrier, inc=1, device_id=(tm, sy, 1 - sx), device_id_type=MESH)
        local().start()

    @pl.when(step == ENTERED)
    def _():
        pl.semaphore_wait(pltpu.get_barrier_semaphore(), len(PARTNERS) + 1)
        for n in range(len(PARTNERS)):
            copy(n).start()

    @pl.when(step < WEIGHT_STEPS)
    def _():
        weight_block(w1_ref, u1_ref)

    @pl.when(step >= WEIGHT_STEPS)
    def _():
        weight_block(w2_ref, u2_ref)

    @pl.when(step == WEIGHT_STEPS)
    def _():
        local().wait()
        for n in range(len(PARTNERS)):
            copy(n).wait()
        across().start()

    @pl.when(step == LAST)
    def _():
        across().wait()


def gathered(own, first_kernel, second_kernel):
    chunk = C // 3
    hbm = pl.BlockSpec(memory_space=pl.ANY)

    def spec(shape, lead, shift):
        def index(step):
            block = jnp.clip(step - shift, 0, WEIGHT_STEPS - 1)
            return (0,) * lead + (block // 3, block % 3, 0)

        return pl.BlockSpec(shape, index)

    copies = len(PARTNERS)
    sets = jax.ShapeDtypeStruct((SETS, 3, C, C), BF)
    return pl.pallas_call(
        gather_kernel,
        grid=(LAST + 1,),
        in_specs=[
            hbm,
            spec((3, 3, 1, chunk, C), 2, 0),
            spec((3, 3, 1, chunk, C), 2, WEIGHT_STEPS),
        ],
        out_specs=[
            hbm,
            spec((SETS, 1, chunk, C), 1, 0),
            spec((SETS, 1, chunk, C), 1, WEIGHT_STEPS),
        ],
        out_shape=[jax.ShapeDtypeStruct((SOURCES, 2, BAND, 16, 128), BF), sets, sets],
        scratch_shapes=[
            pltpu.SemaphoreType.DMA((copies,)),
            pltpu.SemaphoreType.DMA((copies,)),
            pltpu.SemaphoreType.DMA,
            pltpu.SemaphoreType.DMA((2,)),
        ],
        compiler_params=pltpu.CompilerParams(
            vmem_limit_bytes=62 * MIB, collective_id=0, has_side_effects=True
        ),
        cost_estimate=pl.CostEstimate(
            flops=60 * 9 * C * C, bytes_accessed=2 * 41 * 3 * C * C * 2, transcendentals=0
        ),
        name="gather",
    )(own, first_kernel, second_kernel)


WIDE = 40
LEAD = 9
SPAN = 16
CELLS = 256
USED = 6 * 2 * SPAN + 24
INNER = 6 * 2 * SPAN
R1 = ROWS + 4
R2 = ROWS + 2
I1 = R2 // 2
I2 = ROWS // 2
HALO_ROWS = 32
ENTRY_ROWS = 4
QUARTER = 4


def norm_act(values, gain, keep):
    mean = jnp.mean(values * values, axis=-1, keepdims=True)
    half = values * (lax.rsqrt(mean + 1e-6) * keep) * gain
    return half * jnp.tanh(half) + half


def shifted(values, edge, ahead):
    line = lax.broadcasted_iota(jnp.int32, values.shape, 0)
    if ahead:
        return jnp.where(line == SPAN - 1, edge, pltpu.roll(values, SPAN - 1, axis=0))
    return jnp.where(line == 0, edge, pltpu.roll(values, 1, axis=0))


def clip_scalars(lengths, first, count):
    found = [jnp.int32(0)] * count
    start = jnp.int32(0)
    for k in range(lengths.shape[0]):
        for n in range(count):
            t = first + n
            found[n] = jnp.where(start <= t, t - start, found[n])
        start = start + lengths[k]
    return found


def spread_latents(all_ref, q_ref, distance, sx, top, bottom):
    depth = SOURCES * 2 * 128
    index = lax.broadcasted_iota(jnp.int32, (depth, 1), 0)
    source = index // 256
    side = (index // 128) % 2
    half = (index // 64) % 2
    frame = (index // 32) % 2
    x = index % 32
    column = jnp.where(side == sx, x, jnp.where(sx == 0, x + COLS, x - COLS))
    wanted = (column >= -HALO) & (column < COLS + HALO)
    target = (2 * source + frame) * WIDE + column + LEAD + 1
    lane = lax.broadcasted_iota(jnp.int32, (depth, 384), 1)
    spread = []
    for h in range(2):
        to = jnp.where(wanted & (half == h), target, -1)
        pick = jnp.where(lane == to, 1.0, 0.0).astype(BF)
        bands = (0, 16 + HALO) if h else (HALO, BAND)
        rows = (bands[1] - bands[0]) * 16
        lhs = jnp.concatenate(
            [
                all_ref[t, s, bands[0] : bands[1]].reshape(rows, 128)
                for t in range(SOURCES)
                for s in range(2)
            ],
            axis=1,
        )
        spread.append(jnp.dot(lhs, pick, preferred_element_type=F32))
    lower, upper = spread
    edge = HALO * 16
    pt = jnp.concatenate(
        [
            upper[:edge] * top.astype(F32),
            lower[: 16 * 16],
            upper[edge:],
            lower[16 * 16 :] * bottom.astype(F32),
        ],
        axis=0,
    )
    pt = pt.astype(BF)
    cell = lax.broadcasted_iota(jnp.int32, (1, CELLS), 1)
    beyond = cell - INNER
    halo = beyond // 6
    frame_of = jnp.where(cell < INNER, cell // 32, beyond - 6 * halo)
    column = jnp.where(
        cell < INNER,
        2 * (cell % SPAN) + (cell // SPAN) % 2,
        jnp.where(halo < 2, halo - 2, COLS + halo - 2),
    )
    base = frame_of * WIDE + column + LEAD
    line = lax.broadcasted_iota(jnp.int32, (384, CELLS), 0)
    for lag in range(3):
        keep = jnp.zeros((1, CELLS), jnp.int32)
        for f in range(6):
            keep = jnp.where(frame_of == f, (distance[f] >= lag).astype(jnp.int32), keep)
        keep = jnp.where(cell < USED, keep, 0)
        for dx in range(3):
            to = jnp.where(keep == 1, base + (2 - lag) * WIDE + dx, -1)
            pick = jnp.where(line == to, 1.0, 0.0).astype(BF)
            q_ref[3 * lag + dx] = jnp.dot(pt, pick, preferred_element_type=F32).astype(BF)


def main_kernel(
    lengths, all_ref, we_ref, g1_ref, g2_ref, w1_hbm, w2_hbm, u1_hbm, u2_hbm,
    out_ref,
    q_ref, f_ref, h_ref, s_ref, e_ref, xa_ref, xb_ref, hxa_ref, hxb_ref, ma_ref, mb_ref, acc_ref,
    w_ref, a_ref, b_ref, hn_ref, keep_ref, sem,
):
    tm = lax.axis_index("tm")
    sy = lax.axis_index("sy")
    sx = lax.axis_index("sx")
    top = (sy > 0).astype(jnp.int32)
    bottom = (sy < lax.axis_size("sy") - 1).astype(jnp.int32)
    left = sx == 0
    distance = clip_scalars(lengths, 2 * tm - 4, 6)
    x_refs, hx_refs, m_refs = (xa_ref, xb_ref), (hxa_ref, hxb_ref), (ma_ref, mb_ref)

    def pair_of(step):
        n = (0, 1, 1)[step // 4]
        whole = distance[3 + 2 * n] >= 1
        return (
            (distance[2 + 2 * n] >= 2).astype(F32),
            (distance[2 + 2 * n] >= 1).astype(F32),
            whole.astype(F32),
            whole,
        )

    def weight_copies(step):
        slot, tau = step % 2, step % 4
        w_hbm, u_hbm = (w1_hbm, u1_hbm) if step < 8 else (w2_hbm, u2_hbm)
        whole = pair_of(step)[3]
        which = (0, jnp.where(whole, 1, 4), jnp.where(whole, 2, 3), 3)[tau]
        mixed = pltpu.make_async_copy(
            u_hbm.at[pl.ds(2 * which, 2)], w_ref.at[slot, pl.ds(1, 2)], sem.at[slot, 0]
        )

        def outer(source, n):
            return pltpu.make_async_copy(source, w_ref.at[slot, 3 * n], sem.at[slot, 1 + n])

        tap = (0, 1, 2, 2)[tau]
        plain = [outer(w_hbm.at[tap, 2 * n], n) for n in range(2)]
        made = None
        if tau in (1, 2):
            made = [outer(u_hbm.at[8 + 2 * tau + n], n) for n in range(2)]
        return whole, mixed, plain, made

    def fetch(step):
        whole, mixed, plain, made = weight_copies(step)
        mixed.start()
        if made is None:
            for one in plain:
                one.start()
            return

        @pl.when(whole)
        def _():
            for one in made:
                one.start()

        @pl.when(jnp.logical_not(whole))
        def _():
            for one in plain:
                one.start()

    def arrive(step):
        _, mixed, plain, _ = weight_copies(step)
        mixed.wait()
        for one in plain:
            one.wait()

    fetch(0)
    spread_latents(all_ref, q_ref, distance, sx, top, bottom)
    cell = lax.broadcasted_iota(jnp.int32, (USED, 128), 0)
    off_left = (cell >= INNER) & (cell < INNER + 12)
    off_right = cell >= INNER + 12
    keep_ref[...] = jnp.where((off_left & left) | (off_right & (sx == 1)), 0.0, 1.0)
    first_gain = g1_ref[...][None, :] * 0.5
    second_gain = g2_ref[...][None, :] * 0.5
    h_ref[...] = jnp.zeros_like(h_ref)

    @pl.loop(0, R1 // ENTRY_ROWS)
    def _(block):
        cols = []
        for n in range(ENTRY_ROWS):
            first = pl.multiple_of((block * ENTRY_ROWS + n) * 16, 16)
            cols.append(
                jnp.concatenate(
                    [
                        q_ref[3 * lag + dx, pl.ds(first + 16 * dy, 16), :]
                        for lag in (2, 1, 0)
                        for dy in range(3)
                        for dx in range(3)
                    ],
                    axis=0,
                )
            )
        patches = jnp.concatenate(cols, axis=1)
        entry = lax.dot_general(
            patches, we_ref[...], (((0,), (0,)), ((), ())), preferred_element_type=F32
        ).astype(BF)
        for n in range(ENTRY_ROWS):
            row = block * ENTRY_ROWS + n
            inside = jnp.where(row < 2, top, jnp.where(row >= R1 - 2, bottom, 1)).astype(F32)
            value = entry[n * CELLS : n * CELLS + USED].astype(F32)
            for f in range(2):
                e_ref[f, row] = entry[n * CELLS + (4 + f) * 32 : n * CELLS + (5 + f) * 32]
            a_ref[n] = norm_act(value, first_gain, keep_ref[:, :1] * inside)
        for n in range(ENTRY_ROWS):
            row = block * ENTRY_ROWS + n
            for f in range(6):
                even = a_ref[n, f * 32 : f * 32 + SPAN, :]
                odd = a_ref[n, f * 32 + SPAN : f * 32 + 2 * SPAN, :]
                before = a_ref[n, INNER + 6 + f : INNER + 7 + f, :]
                after = a_ref[n, INNER + 12 + f : INNER + 13 + f, :]
                f_ref[f, row, 0] = shifted(odd, before, False).astype(BF)
                f_ref[f, row, 1] = even.astype(BF)
                f_ref[f, row, 2] = odd.astype(BF)
                f_ref[f, row, 3] = shifted(even, after, True).astype(BF)
                places = (
                    jnp.where(left, f * 32 + 31, INNER + f),
                    jnp.where(left, INNER + 12 + f, INNER + 6 + f),
                    jnp.where(left, INNER + 18 + f, f * 32),
                )
                for dx, place in enumerate(places):
                    h_ref[f, n % 2, pl.ds(row // 2, 1), dx * C : (dx + 1) * C] = a_ref[
                        n, pl.ds(place, 1), :
                    ]

    def time_mix(step, one, dtype):
        tau = step % 4
        k0, k1, s, _ = pair_of(step)
        base = 2 if 4 <= step < 8 else 0

        def scaled(value, by):
            if dtype == F32:
                return value * by
            tile = jnp.full((16, 128), by, F32).astype(BF)
            return value * jnp.tile(tile, (1, value.shape[1] // 128))

        if tau == 0:
            return scaled(one(base), k0) - scaled(one(base + 2), s)
        if tau == 1:
            return scaled(one(base + 1), k1) + scaled(one(base + 2), s)
        if tau == 2:
            return one(base + 2) - scaled(one(base + 1), s * k1)
        return scaled(one(base + 1), s * k1) - one(base + 3)

    def row_transform(d):
        return d[0] - d[2], d[1] + d[2], d[2] - d[1], d[1] - d[3]

    def build(step, i):
        source = f_ref if step < 8 else s_ref
        x_ref = x_refs[step % 2]
        for j in range(4):
            d = [
                time_mix(step, lambda frame, k=k: source[frame, 2 * i + k, j], BF)
                for k in range(4)
            ]
            for k, value in enumerate(row_transform(d)):
                x_ref[k, j, pl.ds(pl.multiple_of(i * SPAN, SPAN), SPAN), :] = value

    def build_halo(step):
        hx_ref = hx_refs[step % 2]
        for dx in range(3):
            lanes = slice(dx * C, (dx + 1) * C)
            d = [
                time_mix(
                    step,
                    lambda frame, k=k: h_ref[frame, k % 2, pl.ds(k // 2, HALO_ROWS), lanes],
                    F32,
                )
                for k in range(4)
            ]
            for k, value in enumerate(row_transform(d)):
                hx_ref[k, :, lanes] = value.astype(BF)

    def settle(step, part):
        tau = step % 4
        m_ref = m_refs[step % 2]
        s = pair_of(step)[2]
        t = [m_ref[k, part, :] for k in range(4)]
        middle = t[1] - t[2]
        both = (t[0] + t[1] + t[2], middle - t[3])
        if tau == 3:
            return 1, [acc_ref[1, p, part, :] - both[p] for p in range(2)]
        if tau == 2:
            for p in range(2):
                acc_ref[1, p, part, :] = acc_ref[1, p, part, :] - s * both[p]
            return 0, [acc_ref[0, p, part, :] + both[p] for p in range(2)]
        for p in range(2):
            if tau == 0:
                acc_ref[0, p, part, :] = both[p]
            else:
                acc_ref[0, p, part, :] = acc_ref[0, p, part, :] + both[p]
                acc_ref[1, p, part, :] = s * both[p]
        return None

    def settle_halo(step):
        done = settle(step, pl.ds(2 * I1 * SPAN, HALO_ROWS))
        if done is not None:
            for p, value in enumerate(done[1]):
                hn_ref[p] = norm_act(value, second_gain, 1.0)

    def settle_first(step, i):
        for side in range(2):
            first = pl.multiple_of(side * I1 * SPAN + i * SPAN, SPAN)
            done = settle(step, pl.ds(first, SPAN))
            if done is None:
                continue
            frame = 2 * (step // 4) + done[0]
            for p, value in enumerate(done[1]):
                row = 2 * i + p
                inside = jnp.where(row == 0, top, jnp.where(row == R2 - 1, bottom, 1)).astype(F32)
                value = norm_act(value, second_gain, inside)
                here = inside * jnp.where(sx == side, 1.0, 0.0)
                edge = hn_ref[p, pl.ds(i, 1), :] * here
                if side == 0:
                    s_ref[frame, row, 1] = value.astype(BF)
                    s_ref[frame, row, 3] = shifted(value, edge, True).astype(BF)
                else:
                    s_ref[frame, row, 2] = value.astype(BF)
                    s_ref[frame, row, 0] = shifted(value, edge, False).astype(BF)

    def settle_second(step, i, n):
        done = [
            settle(step, pl.ds(pl.multiple_of(side * I2 * SPAN + i * SPAN, SPAN), SPAN))
            for side in range(2)
        ]
        if done[0] is None:
            return
        member = done[0][0]
        for p in range(2):
            row = 2 * i + p
            for side in range(2):
                part = slice(side * SPAN, (side + 1) * SPAN)
                value = done[side][1][p] + e_ref[member, row + 2, part, :].astype(F32)
                for lane in range(3):
                    b_ref[2 * n + p, lane, pl.ds(side, SPAN, stride=2), :] = value[
                        :, lane * 128 : (lane + 1) * 128
                    ]
            for lane in range(3):
                out_ref[member, row, :, lane * 128 : (lane + 1) * 128] = b_ref[
                    2 * n + p, lane
                ].astype(BF)

    def products(step, k):
        x_ref, m_ref = x_refs[step % 2], m_refs[step % 2]
        count = (I1 if step < 8 else I2) * SPAN
        x = [x_ref[k, j, :count, :] for j in range(4)]
        parts = [jnp.concatenate(x[:3], axis=1), jnp.concatenate(x[1:], axis=1)]
        if step < 8:
            parts.append(hx_refs[step % 2][k])
        lhs = jnp.concatenate(parts, axis=0)
        m_ref[k, : lhs.shape[0], :] = jnp.dot(
            lhs, w_ref[step % 2, k], preferred_element_type=F32
        )

    def build_alone(step):
        @pl.loop(0, I1 if step < 8 else I2)
        def _(i):
            build(step, i)

        if step < 8:
            build_halo(step)

    def run(step):
        arrive(step)
        if step < 11:
            fetch(step + 1)
        builds = step not in (7, 11)
        settles = step not in (0, 8)
        if builds and step < 8:
            build(step + 1, I1 - 1)
            build_halo(step + 1)
        if settles and step < 8:
            settle_halo(step - 1)
            settle_first(step - 1, I1 - 1)

        @pl.loop(0, 4)
        def _(k):
            products(step, k)
            for n in range(QUARTER):
                i = QUARTER * k + n
                if builds:
                    build(step + 1, i)
                if settles:
                    if step < 8:
                        settle_first(step - 1, i)
                    else:
                        settle_second(step - 1, i, n)

    build_alone(0)
    for step in range(8):
        run(step)
    settle_halo(7)

    @pl.loop(0, I1)
    def _(i):
        settle_first(7, i)

    build_alone(8)
    for step in range(8, 12):
        run(step)

    @pl.loop(0, 4)
    def _(k):
        for n in range(QUARTER):
            settle_second(11, QUARTER * k + n, n)


def block_call(*operands):
    vmem = pl.BlockSpec(memory_space=pltpu.VMEM)
    smem = pl.BlockSpec(memory_space=pltpu.SMEM)
    hbm = pl.BlockSpec(memory_space=pl.ANY)
    m1 = 2 * I1 * SPAN + HALO_ROWS
    return pl.pallas_call(
        main_kernel,
        in_specs=[smem, vmem, vmem, vmem, vmem, hbm, hbm, hbm, hbm],
        out_specs=vmem,
        out_shape=jax.ShapeDtypeStruct((2, ROWS, COLS, C), BF),
        scratch_shapes=[
            pltpu.VMEM((9, 38 * 16, CELLS), BF),
            pltpu.VMEM((6, R1, 4, SPAN, C), BF),
            pltpu.VMEM((6, 2, HALO_ROWS + 8, K3), F32),
            pltpu.VMEM((4, R2, 4, SPAN, C), BF),
            pltpu.VMEM((2, R1, COLS, C), BF),
            pltpu.VMEM((4, 4, I1 * SPAN, C), BF),
            pltpu.VMEM((4, 4, I1 * SPAN, C), BF),
            pltpu.VMEM((4, HALO_ROWS, K3), BF),
            pltpu.VMEM((4, HALO_ROWS, K3), BF),
            pltpu.VMEM((4, m1, C), F32),
            pltpu.VMEM((4, m1, C), F32),
            pltpu.VMEM((2, 2, m1, C), F32),
            pltpu.VMEM((2, 4, K3, C), BF),
            pltpu.VMEM((ENTRY_ROWS, USED, C), F32),
            pltpu.VMEM((2 * QUARTER, 3, COLS, 128), F32),
            pltpu.VMEM((2, HALO_ROWS, C), F32),
            pltpu.VMEM((USED, 128), F32),
            pltpu.SemaphoreType.DMA((2, 3)),
        ],
        compiler_params=pltpu.CompilerParams(vmem_limit_bytes=62 * MIB),
        name="block",
    )(*operands)


def body(latent, clip_lengths, entry_kernel, first_gain, first_kernel, second_gain, second_kernel):
    own = latent.reshape(2, 2, 16, COLS, 16).transpose(2, 4, 1, 0, 3).reshape(16, 16, 128)
    everything, u1, u2 = gathered(own, first_kernel, second_kernel)
    return block_call(
        clip_lengths,
        everything,
        entry_kernel.reshape(27 * 16, C),
        first_gain,
        second_gain,
        first_kernel.reshape(3, 3, K3, C),
        second_kernel.reshape(3, 3, K3, C),
        u1.reshape(SETS, K3, C),
        u2.reshape(SETS, K3, C),
    )


def solution(mesh):
    return jax.shard_map(
        body,
        mesh=mesh,
        in_specs=(P("tm", "sy", "sx", None), P(), P(), P(), P(), P(), P()),
        out_specs=P("tm", "sy", "sx", None),
        check_vma=False,
    )
```

time: 123 us -> 106 us (0.86); the launches traced: 123 us -> 104 us
  Pallas kernels: 121 us -> 102 us
    pallas_call x1, Pallas kernels: 90.4 us -> 73.8 us  [block_call(): pl.pallas_call(main_kernel, in_specs=[smem, vmem, vmem, vmem, vmem, hbm,...]
    pallas_call x1, Pallas kernels: 30.4 us -> 28 us  [gathered(): pl.pallas_call(gather_kernel, grid=(LAST + 1,), in_specs=[hbm, spec((3, 3...]
where the time goes in v2:
time: 106 us; the launch traced here: 104 us
  Pallas kernels  102 us (96%)
  local copies, waits for them, and re-layouts  2.02 us (2%)
    pallas_call x1, Pallas kernels, block_call(): pl.pallas_call(main_kernel, in_specs=[smem, vmem, vmem, vmem, vmem, hbm,...  73.8 us
    pallas_call x1, Pallas kernels, gathered(): pl.pallas_call(gather_kernel, grid=(LAST + 1,), in_specs=[hbm, spec((3, 3...  28 us

profile of v2, /device:TPU:1, one launch (start us, length us, event | category | flops | bytes accessed | tf_op | source)
XLA Modules:
  0.0 104.0 jit_solution(17844881345954536597)
XLA Ops:
  0.0 1.2 %copy.10 = bf16[2,2,16,32,16]{3,0,1,4,2:T(2,128)(2,1)S(1)} copy(bf16[2,2,16,32,16]{3,4,2,1,0:T(8,128)(2,1)} %bitcast.15) | data formatting | bytes 131072 | tf_op jit(solution)/shard_map/reshape | solution.py:617
  1.2 0.8 reshape.22.own_ref
  2.0 28.0 %gather.1 = (bf16[4,2,22,16,128]{4,3,2,1,0:T(8,128)(2,1)}, bf16[14,3,384,384]{3,2,1,0:T(8,128)(2,1)}, bf16[14,3,384,384]{3,2,1,0:T(8,128)(2,1)}) custom-call(bf16[16,16,128]{2,1,0:T(8,128)(2,1)} %reshape.22.own_ref, bf16[3,3,3,384,384]{4,3,2,1,0:T(8,128)(2,1)} %w1_ref.1, bf16[3,3,3,384,384]{4,3,2,1,0:T(8,128)(2,1)} %w2_ref.1), custom_call_target="tpu_custom_call" | custom-call | flops 79626240 | bytes 72548352 | tf_op jit(solution)/shard_map/gather/pallas_call | solution.py:143
  30.0 73.8 %block.1 = bf16[2,32,32,384]{3,2,1,0:T(8,128)(2,1)} custom-call(s32[9]{0:T(128)} %lengths.1, bf16[4,2,22,16,128]{4,3,2,1,0:T(8,128)(2,1)} %get-tuple-element.8.all_ref, bf16[432,384]{1,0:T(8,128)(2,1)} %bitcast.14, f32[384]{0:T(512)} %g1_ref.1, f32[384]{0:T(512)} %g2_ref.1, bf16[3,3,1152,384]{3,2,1,0:T(8,128)(2,1)} %bitcast.9, ...), custom_call_target="tpu_custom_call" | custom-call | tf_op jit(solution)/shard_map/block/pallas_call | solution.py:586

commit v3 on v2

--- a/solution.py
+++ b/solution.py
@@ -21,12 +21,31 @@
 BAND = 16 + 2 * HALO
 SOURCES = 4
 WEIGHT_STEPS = 9
-LAST = 2 * WEIGHT_STEPS - 1
+LAST = WEIGHT_STEPS - 1
 PARTNERS = [(k, d) for k in range(SOURCES) for d in (0, 1, -1) if (k, d) != (0, 0)]
 SENT = {0: (0, 16), 1: (16 - HALO, HALO), -1: (0, HALO)}
 LANDS = {0: HALO, 1: 0, -1: HALO + 16}
 SETS = 14
-ENTERED = 2
+ENTERED = 1
+LANDED = 5
+
+
+def mix_weights(w, put):
+    edge = [w[0][y] + w[2][y] for y in range(3)]
+    times = [
+        w[0],
+        [(edge[y] + w[1][y]) * 0.5 for y in range(3)],
+        [(edge[y] - w[1][y]) * 0.5 for y in range(3)],
+        w[2],
+        w[1],
+    ]
+    for t, g in enumerate(times):
+        outer = g[0] + g[2]
+        put(2 * t, (outer + g[1]) * 0.5)
+        put(2 * t + 1, (outer - g[1]) * 0.5)
+    for n, t in enumerate((1, 2)):
+        put(10 + 2 * n, times[t][0])
+        put(11 + 2 * n, times[t][2])
 
 
 def weight_block(w_ref, u_ref):
@@ -35,26 +54,18 @@
     @pl.loop(0, w_ref.shape[3] // step)
     def _(block):
         part = pl.ds(pl.multiple_of(block * step, step), step)
-        w = [[w_ref[t, y, 0, part, :].astype(F32) for y in range(3)] for t in range(3)]
-        edge = [w[0][y] + w[2][y] for y in range(3)]
-        times = [
-            w[0],
-            [(edge[y] + w[1][y]) * 0.5 for y in range(3)],
-            [(edge[y] - w[1][y]) * 0.5 for y in range(3)],
-            w[2],
-            w[1],
-        ]
-        for t, g in enumerate(times):
-            outer = g[0] + g[2]
-            u_ref[2 * t, 0, part, :] = ((outer + g[1]) * 0.5).astype(BF)
-            u_ref[2 * t + 1, 0, part, :] = ((outer - g[1]) * 0.5).astype(BF)
-        for n, t in enumerate((1, 2)):
-            u_ref[10 + 2 * n, 0, part, :] = times[t][0].astype(BF)
-            u_ref[11 + 2 * n, 0, part, :] = times[t][2].astype(BF)
+        for lane in range(3):
+            lanes = slice(lane * 128, (lane + 1) * 128)
+            w = [[w_ref[t, y, 0, part, lanes].astype(F32) for y in range(3)] for t in range(3)]
+
+            def put(n, value, lanes=lanes):
+                u_ref[n, 0, part, lanes] = value.astype(BF)
+
+            mix_weights(w, put)
 
 
 def gather_kernel(
-    own_ref, w1_ref, w2_ref, all_ref, u1_ref, u2_ref, send_sem, recv_sem, local_sem, pair_sem
+    own_ref, w1_ref, all_ref, u1_ref, send_sem, recv_sem, local_sem, pair_sem
 ):
     step = pl.program_id(0)
     tm = lax.axis_index("tm")
@@ -107,15 +118,9 @@
         for n in range(len(PARTNERS)):
             copy(n).start()
 
-    @pl.when(step < WEIGHT_STEPS)
-    def _():
-        weight_block(w1_ref, u1_ref)
-
-    @pl.when(step >= WEIGHT_STEPS)
-    def _():
-        weight_block(w2_ref, u2_ref)
-
-    @pl.when(step == WEIGHT_STEPS)
+    weight_block(w1_ref, u1_ref)
+
+    @pl.when(step == LANDED)
     def _():
         local().wait()
         for n in range(len(PARTNERS)):
@@ -127,33 +132,25 @@
         across().wait()
 
 
-def gathered(own, first_kernel, second_kernel):
+def gathered(own, first_kernel):
     chunk = C // 3
     hbm = pl.BlockSpec(memory_space=pl.ANY)
-
-    def spec(shape, lead, shift):
-        def index(step):
-            block = jnp.clip(step - shift, 0, WEIGHT_STEPS - 1)
-            return (0,) * lead + (block // 3, block % 3, 0)
-
-        return pl.BlockSpec(shape, index)
-
     copies = len(PARTNERS)
-    sets = jax.ShapeDtypeStruct((SETS, 3, C, C), BF)
     return pl.pallas_call(
         gather_kernel,
-        grid=(LAST + 1,),
+        grid=(WEIGHT_STEPS,),
         in_specs=[
             hbm,
-            spec((3, 3, 1, chunk, C), 2, 0),
-            spec((3, 3, 1, chunk, C), 2, WEIGHT_STEPS),
+            pl.BlockSpec((3, 3, 1, chunk, C), lambda step: (0, 0, step // 3, step % 3, 0)),
         ],
         out_specs=[
             hbm,
-            spec((SETS, 1, chunk, C), 1, 0),
-            spec((SETS, 1, chunk, C), 1, WEIGHT_STEPS),
+            pl.BlockSpec((SETS, 1, chunk, C), lambda step: (0, step // 3, step % 3, 0)),
         ],
-        out_shape=[jax.ShapeDtypeStruct((SOURCES, 2, BAND, 16, 128), BF), sets, sets],
+        out_shape=[
+            jax.ShapeDtypeStruct((SOURCES, 2, BAND, 16, 128), BF),
+            jax.ShapeDtypeStruct((SETS, 3, C, C), BF),
+        ],
         scratch_shapes=[
             pltpu.SemaphoreType.DMA((copies,)),
             pltpu.SemaphoreType.DMA((copies,)),
@@ -164,10 +161,10 @@
             vmem_limit_bytes=62 * MIB, collective_id=0, has_side_effects=True
         ),
         cost_estimate=pl.CostEstimate(
-            flops=60 * 9 * C * C, bytes_accessed=2 * 41 * 3 * C * C * 2, transcendentals=0
+            flops=60 * 9 * C * C, bytes_accessed=41 * 3 * C * C * 2, transcendentals=0
         ),
         name="gather",
-    )(own, first_kernel, second_kernel)
+    )(own, first_kernel)
 
 
 WIDE = 40
@@ -183,11 +180,25 @@
 HALO_ROWS = 32
 ENTRY_ROWS = 4
 QUARTER = 4
+QUARTERS = 4
+PIECE = 48
+PIECES = K3 // PIECE
+AHEAD = 3
 
 
 def norm_act(values, gain, keep):
     mean = jnp.mean(values * values, axis=-1, keepdims=True)
     half = values * (lax.rsqrt(mean + 1e-6) * keep) * gain
+    return half * jnp.tanh(half) + half
+
+
+def norm_act_wide(values, gain, keep):
+    squares = values * values
+    folded = squares[:, :128] + squares[:, 128:256] + squares[:, 256:]
+    ones = jnp.full((128, 128), 1.0, BF)
+    mean = jnp.dot(folded.astype(BF), ones, preferred_element_type=F32) * (1.0 / C)
+    scale = lax.rsqrt(mean + 1e-6) * keep
+    half = values * jnp.concatenate([scale] * 3, axis=1) * gain
     return half * jnp.tanh(half) + half
 
 
@@ -271,10 +282,10 @@
 
 
 def main_kernel(
-    lengths, all_ref, we_ref, g1_ref, g2_ref, w1_hbm, w2_hbm, u1_hbm, u2_hbm,
-    out_ref,
-    q_ref, f_ref, h_ref, s_ref, e_ref, xa_ref, xb_ref, hxa_ref, hxb_ref, ma_ref, mb_ref, acc_ref,
-    w_ref, a_ref, b_ref, hn_ref, keep_ref, sem,
+    lengths, all_ref, we_ref, g1_ref, g2_ref, w1_hbm, w2_hbm, u1_hbm,
+    out_ref, u2_hbm,
+    q_ref, f_ref, h_ref, s0_ref, s1_ref, s2_ref, s3_ref, e_ref, xa_ref, xb_ref, hxa_ref, hxb_ref, ma_ref, mb_ref, acc_ref,
+    w_ref, a_ref, b_ref, hn_ref, keep_ref, raw_ref, made_ref, sem, raw_sem, made_sem,
 ):
     tm = lax.axis_index("tm")
     sy = lax.axis_index("sy")
@@ -283,6 +294,7 @@
     bottom = (sy < lax.axis_size("sy") - 1).astype(jnp.int32)
     left = sx == 0
     distance = clip_scalars(lengths, 2 * tm - 4, 6)
+    s_refs = (s0_ref, s1_ref, s2_ref, s3_ref)
     x_refs, hx_refs, m_refs = (xa_ref, xb_ref), (hxa_ref, hxb_ref), (ma_ref, mb_ref)
 
     def pair_of(step):
@@ -338,7 +350,49 @@
         for one in plain:
             one.wait()
 
+    def raw_copy(piece, slot):
+        part = pl.ds(pl.multiple_of(piece * PIECE, PIECE), PIECE)
+        return pltpu.make_async_copy(w2_hbm.at[:, :, part], raw_ref.at[slot], raw_sem.at[slot])
+
+    def made_copy(piece, slot):
+        part = pl.ds(pl.multiple_of(piece * PIECE, PIECE), PIECE)
+        return pltpu.make_async_copy(made_ref.at[slot], u2_hbm.at[:, part], made_sem.at[slot])
+
+    def piece_in(step, k):
+        piece = QUARTERS * step + k
+        raw_copy(piece, k).wait()
+        if step > 0:
+            made_copy(piece - QUARTERS, k).wait()
+        if step < PIECES // QUARTERS - 1:
+            raw_copy(piece + AHEAD, lax.rem(k + AHEAD, QUARTERS)).start()
+        else:
+
+            @pl.when(k + AHEAD < QUARTERS)
+            def _():
+                raw_copy(piece + AHEAD, lax.rem(k + AHEAD, QUARTERS)).start()
+
+    def piece_made(step, k):
+        slot = k
+        for block in range(PIECE // 16):
+            rows = slice(block * 16, (block + 1) * 16)
+            for lane in range(3):
+                lanes = slice(lane * 128, (lane + 1) * 128)
+                w = [
+                    [raw_ref[slot, t, y, rows, lanes].astype(F32) for y in range(3)]
+                    for t in range(3)
+                ]
+
+                def put(n, value, rows=rows, lanes=lanes):
+                    made_ref[slot, n, rows, lanes] = value.astype(BF)
+
+                mix_weights(w, put)
+
+    def piece_out(step, k):
+        made_copy(QUARTERS * step + k, k).start()
+
     fetch(0)
+    for k in range(AHEAD):
+        raw_copy(k, k).start()
     spread_latents(all_ref, q_ref, distance, sx, top, bottom)
     cell = lax.broadcasted_iota(jnp.int32, (USED, 128), 0)
     off_left = (cell >= INNER) & (cell < INNER + 12)
@@ -374,7 +428,7 @@
             value = entry[n * CELLS : n * CELLS + USED].astype(F32)
             for f in range(2):
                 e_ref[f, row] = entry[n * CELLS + (4 + f) * 32 : n * CELLS + (5 + f) * 32]
-            a_ref[n] = norm_act(value, first_gain, keep_ref[:, :1] * inside)
+            a_ref[n] = norm_act_wide(value, first_gain, keep_ref[...] * inside)
         for n in range(ENTRY_ROWS):
             row = block * ENTRY_ROWS + n
             for f in range(6):
@@ -419,11 +473,13 @@
         return d[0] - d[2], d[1] + d[2], d[2] - d[1], d[1] - d[3]
 
     def build(step, i):
-        source = f_ref if step < 8 else s_ref
+        def read(frame, row, j):
+            return f_ref[frame, row, j] if step < 8 else s_refs[frame][row, j]
+
         x_ref = x_refs[step % 2]
         for j in range(4):
             d = [
-                time_mix(step, lambda frame, k=k: source[frame, 2 * i + k, j], BF)
+                time_mix(step, lambda frame, k=k: read(frame, 2 * i + k, j), BF)
                 for k in range(4)
             ]
             for k, value in enumerate(row_transform(d)):
@@ -485,11 +541,11 @@
                 here = inside * jnp.where(sx == side, 1.0, 0.0)
                 edge = hn_ref[p, pl.ds(i, 1), :] * here
                 if side == 0:
-                    s_ref[frame, row, 1] = value.astype(BF)
-                    s_ref[frame, row, 3] = shifted(value, edge, True).astype(BF)
+                    s_refs[frame][row, 1] = value.astype(BF)
+                    s_refs[frame][row, 3] = shifted(value, edge, True).astype(BF)
                 else:
-                    s_ref[frame, row, 2] = value.astype(BF)
-                    s_ref[frame, row, 0] = shifted(value, edge, False).astype(BF)
+                    s_refs[frame][row, 2] = value.astype(BF)
+                    s_refs[frame][row, 0] = shifted(value, edge, False).astype(BF)
 
     def settle_second(step, i, n):
         done = [
@@ -537,42 +593,48 @@
         arrive(step)
         if step < 11:
             fetch(step + 1)
-        builds = step not in (7, 11)
-        settles = step not in (0, 8)
-        if builds and step < 8:
+        builds = step < 11
+        settles = step > 0
+        pieces = step < PIECES // QUARTERS
+        if builds and step < 7:
             build(step + 1, I1 - 1)
             build_halo(step + 1)
-        if settles and step < 8:
+        if settles and step < 9:
             settle_halo(step - 1)
             settle_first(step - 1, I1 - 1)
 
-        @pl.loop(0, 4)
+        @pl.loop(0, QUARTERS)
         def _(k):
+            if pieces:
+                piece_in(step, k)
             products(step, k)
-            for n in range(QUARTER):
+            for n in range(QUARTER if settles else 0):
+                if step < 9:
+                    settle_first(step - 1, QUARTER * k + n)
+                else:
+                    settle_second(step - 1, QUARTER * k + n, n)
+            for n in range(QUARTER if builds else 0):
                 i = QUARTER * k + n
-                if builds:
-                    build(step + 1, i)
-                if settles:
-                    if step < 8:
-                        settle_first(step - 1, i)
-                    else:
-                        settle_second(step - 1, i, n)
-
-    build_alone(0)
-    for step in range(8):
-        run(step)
-    settle_halo(7)
+                build(step + 1, jnp.maximum(i - 1, 0) if step == 7 else i)
+            if pieces:
+                piece_made(step, k)
+                piece_out(step, k)
+
+        if step == PIECES // QUARTERS - 1:
+            for k in range(QUARTERS):
+                made_copy(QUARTERS * step + k, k).wait()
+        if step == 7:
+            build(8, I2 - 1)
 
     @pl.loop(0, I1)
     def _(i):
-        settle_first(7, i)
-
-    build_alone(8)
-    for step in range(8, 12):
+        build(0, i)
+
+    build_halo(0)
+    for step in range(12):
         run(step)
 
-    @pl.loop(0, 4)
+    @pl.loop(0, QUARTERS)
     def _(k):
         for n in range(QUARTER):
             settle_second(11, QUARTER * k + n, n)
@@ -585,14 +647,20 @@
     m1 = 2 * I1 * SPAN + HALO_ROWS
     return pl.pallas_call(
         main_kernel,
-        in_specs=[smem, vmem, vmem, vmem, vmem, hbm, hbm, hbm, hbm],
-        out_specs=vmem,
-        out_shape=jax.ShapeDtypeStruct((2, ROWS, COLS, C), BF),
+        in_specs=[smem, vmem, vmem, vmem, vmem, hbm, hbm, hbm],
+        out_specs=[vmem, hbm],
+        out_shape=[
+            jax.ShapeDtypeStruct((2, ROWS, COLS, C), BF),
+            jax.ShapeDtypeStruct((SETS, K3, C), BF),
+        ],
         scratch_shapes=[
             pltpu.VMEM((9, 38 * 16, CELLS), BF),
             pltpu.VMEM((6, R1, 4, SPAN, C), BF),
             pltpu.VMEM((6, 2, HALO_ROWS + 8, K3), F32),
-            pltpu.VMEM((4, R2, 4, SPAN, C), BF),
+            pltpu.VMEM((R2, 4, SPAN, C), BF),
+            pltpu.VMEM((R2, 4, SPAN, C), BF),
+            pltpu.VMEM((R2, 4, SPAN, C), BF),
+            pltpu.VMEM((R2, 4, SPAN, C), BF),
             pltpu.VMEM((2, R1, COLS, C), BF),
             pltpu.VMEM((4, 4, I1 * SPAN, C), BF),
             pltpu.VMEM((4, 4, I1 * SPAN, C), BF),
@@ -606,16 +674,20 @@
             pltpu.VMEM((2 * QUARTER, 3, COLS, 128), F32),
             pltpu.VMEM((2, HALO_ROWS, C), F32),
             pltpu.VMEM((USED, 128), F32),
+            pltpu.VMEM((QUARTERS, 3, 3, PIECE, C), BF),
+            pltpu.VMEM((QUARTERS, SETS, PIECE, C), BF),
             pltpu.SemaphoreType.DMA((2, 3)),
+            pltpu.SemaphoreType.DMA((QUARTERS,)),
+            pltpu.SemaphoreType.DMA((QUARTERS,)),
         ],
         compiler_params=pltpu.CompilerParams(vmem_limit_bytes=62 * MIB),
         name="block",
-    )(*operands)
+    )(*operands)[0]
 
 
 def body(latent, clip_lengths, entry_kernel, first_gain, first_kernel, second_gain, second_kernel):
     own = latent.reshape(2, 2, 16, COLS, 16).transpose(2, 4, 1, 0, 3).reshape(16, 16, 128)
-    everything, u1, u2 = gathered(own, first_kernel, second_kernel)
+    everything, u1 = gathered(own, first_kernel)
     return block_call(
         clip_lengths,
         everything,
@@ -625,7 +697,6 @@
         first_kernel.reshape(3, 3, K3, C),
         second_kernel.reshape(3, 3, K3, C),
         u1.reshape(SETS, K3, C),
-        u2.reshape(SETS, K3, C),
     )
 
 

time: 106 us -> 94.2 us (0.89); the launches traced: 104 us -> 93.5 us
  Pallas kernels: 102 us -> 91.3 us
    pallas_call x1, Pallas kernels: 28 us -> 19.8 us  [gathered(): pl.pallas_call(gather_kernel, grid=(WEIGHT_STEPS,), in_specs=[hbm, pl.Blo...]
    pallas_call x1, Pallas kernels: 73.8 us -> 71.6 us  [block_call(): pl.pallas_call(main_kernel, in_specs=[smem, vmem, vmem, vmem, vmem, hbm,...]
where the time goes in v3:
time: 94.2 us; the launch traced here: 93.5 us
  Pallas kernels  91.3 us (97%)
  local copies, waits for them, and re-layouts  2.02 us (2%)
    pallas_call x1, Pallas kernels, block_call(): pl.pallas_call(main_kernel, in_specs=[smem, vmem, vmem, vmem, vmem, hbm,...  71.6 us
    pallas_call x1, Pallas kernels, gathered(): pl.pallas_call(gather_kernel, grid=(WEIGHT_STEPS,), in_specs=[hbm, pl.Blo...  19.8 us
    reshape x2, local copies, waits for them, and re-layouts, body(): latent.reshape(2, 2, 16, COLS, 16).transpose(2, 4, 1, 0, 3)  2.02 us

profile of v3, /device:TPU:1, one launch (start us, length us, event | category | flops | bytes accessed | tf_op | source)
XLA Modules:
  0.0 93.5 jit_solution(9232422523940457892)
XLA Ops:
  0.0 1.2 %copy.10 = bf16[2,2,16,32,16]{3,0,1,4,2:T(2,128)(2,1)S(1)} copy(bf16[2,2,16,32,16]{3,4,2,1,0:T(8,128)(2,1)} %bitcast.13) | data formatting | bytes 131072 | tf_op jit(solution)/shard_map/reshape | solution.py:689
  1.2 0.8 reshape.19.own_ref
  2.0 19.8 %gather.1 = (bf16[4,2,22,16,128]{4,3,2,1,0:T(8,128)(2,1)}, bf16[14,3,384,384]{3,2,1,0:T(8,128)(2,1)}) custom-call(bf16[16,16,128]{2,1,0:T(8,128)(2,1)} %reshape.19.own_ref, bf16[3,3,3,384,384]{4,3,2,1,0:T(8,128)(2,1)} %w1_ref.1), custom_call_target="tpu_custom_call" | custom-call | flops 79626240 | bytes 36274176 | tf_op jit(solution)/shard_map/gather/pallas_call | solution.py:139
  21.8 71.6 %block.1 = (bf16[2,32,32,384]{3,2,1,0:T(8,128)(2,1)}, bf16[14,1152,384]{2,1,0:T(8,128)(2,1)}) custom-call(s32[9]{0:T(128)} %lengths.1, bf16[4,2,22,16,128]{4,3,2,1,0:T(8,128)(2,1)} %get-tuple-element.8.all_ref, bf16[432,384]{1,0:T(8,128)(2,1)} %bitcast.12, f32[384]{0:T(512)} %g1_ref.1, f32[384]{0:T(512)} %g2_ref.1, bf16[3,3,1152,384]{3,2,1,0:T(8,128)(2,1)} %bitcast.8, ...), custom_call_target="tpu_custom_call" | custom-call | tf_op jit(solution)/shard_map/block/pallas_call | solution.py:648

commit v4 on v3

--- a/solution.py
+++ b/solution.py
@@ -27,7 +27,7 @@
 LANDS = {0: HALO, 1: 0, -1: HALO + 16}
 SETS = 14
 ENTERED = 1
-LANDED = 5
+LANDED = 6
 
 
 def mix_weights(w, put):
@@ -65,7 +65,7 @@
 
 
 def gather_kernel(
-    own_ref, w1_ref, all_ref, u1_ref, send_sem, recv_sem, local_sem, pair_sem
+    latent_ref, w1_ref, all_ref, u1_ref, own_ref, send_sem, recv_sem, local_sem, pair_sem
 ):
     step = pl.program_id(0)
     tm = lax.axis_index("tm")
@@ -110,6 +110,15 @@
         for k, d in PARTNERS:
             pl.semaphore_signal(barrier, inc=1, device_id=place(-k, -d), device_id_type=MESH)
         pl.semaphore_signal(barrier, inc=1, device_id=(tm, sy, 1 - sx), device_id_type=MESH)
+        line = lax.broadcasted_iota(jnp.int32, (COLS, 128), 0)
+        lane = lax.broadcasted_iota(jnp.int32, (COLS, 128), 1)
+        packed = jnp.zeros((16 * 16, 128), F32)
+        for half in range(2):
+            for f in range(2):
+                to = jnp.where(lane == line + (2 * half + f) * COLS, 1.0, 0.0).astype(BF)
+                rows = latent_ref[f, half * 16 : (half + 1) * 16].reshape(16 * 16, COLS)
+                packed = packed + jnp.dot(rows, to, preferred_element_type=F32)
+        own_ref[...] = packed.astype(BF).reshape(16, 16, 128)
         local().start()
 
     @pl.when(step == ENTERED)
@@ -132,7 +141,7 @@
         across().wait()
 
 
-def gathered(own, first_kernel):
+def gathered(latent, first_kernel):
     chunk = C // 3
     hbm = pl.BlockSpec(memory_space=pl.ANY)
     copies = len(PARTNERS)
@@ -140,7 +149,7 @@
         gather_kernel,
         grid=(WEIGHT_STEPS,),
         in_specs=[
-            hbm,
+            pl.BlockSpec(memory_space=pltpu.VMEM),
             pl.BlockSpec((3, 3, 1, chunk, C), lambda step: (0, 0, step // 3, step % 3, 0)),
         ],
         out_specs=[
@@ -152,6 +161,7 @@
             jax.ShapeDtypeStruct((SETS, 3, C, C), BF),
         ],
         scratch_shapes=[
+            pltpu.VMEM((16, 16, 128), BF),
             pltpu.SemaphoreType.DMA((copies,)),
             pltpu.SemaphoreType.DMA((copies,)),
             pltpu.SemaphoreType.DMA,
@@ -164,7 +174,7 @@
             flops=60 * 9 * C * C, bytes_accessed=41 * 3 * C * C * 2, transcendentals=0
         ),
         name="gather",
-    )(own, first_kernel)
+    )(latent, first_kernel)
 
 
 WIDE = 40
@@ -178,7 +188,7 @@
 I1 = R2 // 2
 I2 = ROWS // 2
 HALO_ROWS = 32
-ENTRY_ROWS = 4
+ENTRY_ROWS = 12
 QUARTER = 4
 QUARTERS = 4
 PIECE = 48
@@ -283,9 +293,10 @@
 
 def main_kernel(
     lengths, all_ref, we_ref, g1_ref, g2_ref, w1_hbm, w2_hbm, u1_hbm,
-    out_ref, u2_hbm,
+    out_hbm, u2_hbm,
     q_ref, f_ref, h_ref, s0_ref, s1_ref, s2_ref, s3_ref, e_ref, xa_ref, xb_ref, hxa_ref, hxb_ref, ma_ref, mb_ref, acc_ref,
-    w_ref, a_ref, b_ref, hn_ref, keep_ref, raw_ref, made_ref, sem, raw_sem, made_sem,
+    w_ref, a_ref, b_ref, hn_ref, keep_ref, raw_ref, made_ref, out_ref, sem, raw_sem, made_sem,
+    out_sem,
 ):
     tm = lax.axis_index("tm")
     sy = lax.axis_index("sy")
@@ -378,12 +389,12 @@
             for lane in range(3):
                 lanes = slice(lane * 128, (lane + 1) * 128)
                 w = [
-                    [raw_ref[slot, t, y, rows, lanes].astype(F32) for y in range(3)]
+                    [raw_ref[slot, t, y, rows, lanes] for y in range(3)]
                     for t in range(3)
                 ]
 
                 def put(n, value, rows=rows, lanes=lanes):
-                    made_ref[slot, n, rows, lanes] = value.astype(BF)
+                    made_ref[slot, n, rows, lanes] = value
 
                 mix_weights(w, put)
 
@@ -472,7 +483,7 @@
     def row_transform(d):
         return d[0] - d[2], d[1] + d[2], d[2] - d[1], d[1] - d[3]
 
-    def build(step, i):
+    def build(step, i, count=1):
         def read(frame, row, j):
             return f_ref[frame, row, j] if step < 8 else s_refs[frame][row, j]
 
@@ -480,10 +491,12 @@
         for j in range(4):
             d = [
                 time_mix(step, lambda frame, k=k: read(frame, 2 * i + k, j), BF)
-                for k in range(4)
+                for k in range(2 * count + 2)
             ]
-            for k, value in enumerate(row_transform(d)):
-                x_ref[k, j, pl.ds(pl.multiple_of(i * SPAN, SPAN), SPAN), :] = value
+            for n in range(count):
+                part = pl.ds(pl.multiple_of((i + n) * SPAN, SPAN), SPAN)
+                for k, value in enumerate(row_transform(d[2 * n : 2 * n + 4])):
+                    x_ref[k, j, part, :] = value
 
     def build_halo(step):
         hx_ref = hx_refs[step % 2]
@@ -613,9 +626,11 @@
                     settle_first(step - 1, QUARTER * k + n)
                 else:
                     settle_second(step - 1, QUARTER * k + n, n)
-            for n in range(QUARTER if builds else 0):
-                i = QUARTER * k + n
-                build(step + 1, jnp.maximum(i - 1, 0) if step == 7 else i)
+            if step == 7:
+                for n in range(QUARTER):
+                    build(8, jnp.maximum(QUARTER * k + n - 1, 0))
+            elif builds:
+                build(step + 1, QUARTER * k, QUARTER)
             if pieces:
                 piece_made(step, k)
                 piece_out(step, k)
@@ -634,10 +649,22 @@
     for step in range(12):
         run(step)
 
+    first_out = pltpu.make_async_copy(out_ref.at[0], out_hbm.at[0], out_sem.at[QUARTERS])
+    first_out.start()
+
+    def second_out(k):
+        rows = pl.ds(2 * QUARTER * k, 2 * QUARTER)
+        return pltpu.make_async_copy(out_ref.at[1, rows], out_hbm.at[1, rows], out_sem.at[k])
+
     @pl.loop(0, QUARTERS)
     def _(k):
         for n in range(QUARTER):
             settle_second(11, QUARTER * k + n, n)
+        second_out(k).start()
+
+    first_out.wait()
+    for k in range(QUARTERS):
+        second_out(k).wait()
 
 
 def block_call(*operands):
@@ -648,7 +675,7 @@
     return pl.pallas_call(
         main_kernel,
         in_specs=[smem, vmem, vmem, vmem, vmem, hbm, hbm, hbm],
-        out_specs=[vmem, hbm],
+        out_specs=[hbm, hbm],
         out_shape=[
             jax.ShapeDtypeStruct((2, ROWS, COLS, C), BF),
             jax.ShapeDtypeStruct((SETS, K3, C), BF),
@@ -676,9 +703,11 @@
             pltpu.VMEM((USED, 128), F32),
             pltpu.VMEM((QUARTERS, 3, 3, PIECE, C), BF),
             pltpu.VMEM((QUARTERS, SETS, PIECE, C), BF),
+            pltpu.VMEM((2, ROWS, COLS, C), BF),
             pltpu.SemaphoreType.DMA((2, 3)),
             pltpu.SemaphoreType.DMA((QUARTERS,)),
             pltpu.SemaphoreType.DMA((QUARTERS,)),
+            pltpu.SemaphoreType.DMA((QUARTERS + 1,)),
         ],
         compiler_params=pltpu.CompilerParams(vmem_limit_bytes=62 * MIB),
         name="block",
@@ -686,8 +715,7 @@
 
 
 def body(latent, clip_lengths, entry_kernel, first_gain, first_kernel, second_gain, second_kernel):
-    own = latent.reshape(2, 2, 16, COLS, 16).transpose(2, 4, 1, 0, 3).reshape(16, 16, 128)
-    everything, u1 = gathered(own, first_kernel)
+    everything, u1 = gathered(latent.transpose(0, 1, 3, 2), first_kernel)
     return block_call(
         clip_lengths,
         everything,

time: 94.2 us -> 89.3 us (0.948)
  Pallas kernels: 91.3 us -> 88.8 us
  local copies, waits for them, and re-layouts: 2.02 us -> 0 us
    pallas_call x1, Pallas kernels: 71.6 us -> 69.2 us  [block_call(): pl.pallas_call(main_kernel, in_specs=[smem, vmem, vmem, vmem, vmem, hbm,...]
    reshape x2 -> x0, local copies, waits for them, and re-layouts: 2.02 us -> none  [body(): latent.reshape(2, 2, 16, COLS, 16).transpose(2, 4, 1, 0, 3)]
where the time goes in v4:
time: 89.3 us; the launch traced here: 89 us
  Pallas kernels  88.8 us (99%)
    pallas_call x1, Pallas kernels, block_call(): pl.pallas_call(main_kernel, in_specs=[smem, vmem, vmem, vmem, vmem, hbm,...  69.2 us
    pallas_call x1, Pallas kernels, gathered(): pl.pallas_call(gather_kernel, grid=(WEIGHT_STEPS,), in_specs=[pl.BlockSpe...  19.6 us

profile of v4, /device:TPU:1, one launch (start us, length us, event | category | flops | bytes accessed | tf_op | source)
XLA Modules:
  0.0 89.0 jit_solution(6642346906655877955)
XLA Ops:
  0.0 19.6 %gather.1 = (bf16[4,2,22,16,128]{4,3,2,1,0:T(8,128)(2,1)}, bf16[14,3,384,384]{3,2,1,0:T(8,128)(2,1)}) custom-call(bf16[2,32,16,32]{3,2,1,0:T(8,128)(2,1)} %bitcast.9, bf16[3,3,3,384,384]{4,3,2,1,0:T(8,128)(2,1)} %w1_ref.1), custom_call_target="tpu_custom_call" | custom-call | flops 79626240 | bytes 36274176 | tf_op jit(solution)/shard_map/gather/pallas_call | solution.py:148
  19.6 69.2 %block.1 = (bf16[2,32,32,384]{3,2,1,0:T(8,128)(2,1)}, bf16[14,1152,384]{2,1,0:T(8,128)(2,1)}) custom-call(s32[9]{0:T(128)} %lengths.1, bf16[4,2,22,16,128]{4,3,2,1,0:T(8,128)(2,1)} %get-tuple-element.8.all_ref, bf16[432,384]{1,0:T(8,128)(2,1)} %bitcast.8, f32[384]{0:T(512)} %g1_ref.1, f32[384]{0:T(512)} %g2_ref.1, bf16[3,3,1152,384]{3,2,1,0:T(8,128)(2,1)} %bitcast.5, ...), custom_call_target="tpu_custom_call" | custom-call | tf_op jit(solution)/shard_map/block/pallas_call | solution.py:675

commit v5 on v4

--- a/solution.py
+++ b/solution.py
@@ -586,21 +586,31 @@
         x_ref, m_ref = x_refs[step % 2], m_refs[step % 2]
         count = (I1 if step < 8 else I2) * SPAN
         x = [x_ref[k, j, :count, :] for j in range(4)]
-        parts = [jnp.concatenate(x[:3], axis=1), jnp.concatenate(x[1:], axis=1)]
+        even, odd, both = [jnp.concatenate(part, axis=1) for part in (x[:3], x[1:], x)]
         if step < 8:
-            parts.append(hx_refs[step % 2][k])
-        lhs = jnp.concatenate(parts, axis=0)
-        m_ref[k, : lhs.shape[0], :] = jnp.dot(
-            lhs, w_ref[step % 2, k], preferred_element_type=F32
+            halo = hx_refs[step % 2][k]
+            even = jnp.concatenate([even, halo], axis=0)
+            none = jnp.zeros((HALO_ROWS, C), BF)
+            both = jnp.concatenate([both, jnp.concatenate([halo, none], axis=1)], axis=0)
+        slot = step % 2
+        none = jnp.zeros((C, 128), BF)
+        shared = jnp.concatenate(
+            [
+                jnp.concatenate([w_ref[slot, k, :, 256:], none], axis=0),
+                jnp.concatenate([none, w_ref[slot, k, :, :128]], axis=0),
+            ],
+            axis=1,
         )
-
-    def build_alone(step):
-        @pl.loop(0, I1 if step < 8 else I2)
-        def _(i):
-            build(step, i)
-
+        low = jnp.dot(even, w_ref[slot, k, :, :256], preferred_element_type=F32)
+        middle = jnp.dot(both, shared, preferred_element_type=F32)
+        high = jnp.dot(odd, w_ref[slot, k, :, 128:], preferred_element_type=F32)
+        m_ref[k, :count, :256] = low[:count]
+        m_ref[k, :count, 256:] = middle[:count, :128]
+        m_ref[k, count : 2 * count, :128] = middle[:count, 128:]
+        m_ref[k, count : 2 * count, 128:] = high
         if step < 8:
-            build_halo(step)
+            m_ref[k, 2 * count : 2 * count + HALO_ROWS, :256] = low[count:]
+            m_ref[k, 2 * count : 2 * count + HALO_ROWS, 256:] = middle[count:, :128]
 
     def run(step):
         arrive(step)

time: 89.3 us -> 84.3 us (0.944)
  Pallas kernels: 88.8 us -> 83.8 us
    pallas_call x1, Pallas kernels: 69.2 us -> 64.2 us  [block_call(): pl.pallas_call(main_kernel, in_specs=[smem, vmem, vmem, vmem, vmem, hbm,...]
where the time goes in v5:
time: 84.3 us; the launch traced here: 83.9 us
  Pallas kernels  83.8 us (99%)
    pallas_call x1, Pallas kernels, block_call(): pl.pallas_call(main_kernel, in_specs=[smem, vmem, vmem, vmem, vmem, hbm,...  64.2 us
    pallas_call x1, Pallas kernels, gathered(): pl.pallas_call(gather_kernel, grid=(WEIGHT_STEPS,), in_specs=[pl.BlockSpe...  19.6 us

profile of v5, /device:TPU:1, one launch (start us, length us, event | category | flops | bytes accessed | tf_op | source)
XLA Modules:
  0.0 83.9 jit_solution(2615925200631912473)
XLA Ops:
  0.0 19.6 %gather.1 = (bf16[4,2,22,16,128]{4,3,2,1,0:T(8,128)(2,1)}, bf16[14,3,384,384]{3,2,1,0:T(8,128)(2,1)}) custom-call(bf16[2,32,16,32]{3,2,1,0:T(8,128)(2,1)} %bitcast.9, bf16[3,3,3,384,384]{4,3,2,1,0:T(8,128)(2,1)} %w1_ref.1), custom_call_target="tpu_custom_call" | custom-call | flops 79626240 | bytes 36274176 | tf_op jit(solution)/shard_map/gather/pallas_call | solution.py:148
  19.6 64.2 %block.1 = (bf16[2,32,32,384]{3,2,1,0:T(8,128)(2,1)}, bf16[14,1152,384]{2,1,0:T(8,128)(2,1)}) custom-call(s32[9]{0:T(128)} %lengths.1, bf16[4,2,22,16,128]{4,3,2,1,0:T(8,128)(2,1)} %get-tuple-element.8.all_ref, bf16[432,384]{1,0:T(8,128)(2,1)} %bitcast.8, f32[384]{0:T(512)} %g1_ref.1, f32[384]{0:T(512)} %g2_ref.1, bf16[3,3,1152,384]{3,2,1,0:T(8,128)(2,1)} %bitcast.5, ...), custom_call_target="tpu_custom_call" | custom-call | tf_op jit(solution)/shard_map/block/pallas_call | solution.py:685

commit v6 on v5

--- a/solution.py
+++ b/solution.py
@@ -22,7 +22,7 @@
 SOURCES = 4
 WEIGHT_STEPS = 9
 LAST = WEIGHT_STEPS - 1
-PARTNERS = [(k, d) for k in range(SOURCES) for d in (0, 1, -1) if (k, d) != (0, 0)]
+PARTNERS = [(2, 0), (3, 0), (1, 0)] + [(k, d) for k in (2, 3, 1, 0) for d in (1, -1)]
 SENT = {0: (0, 16), 1: (16 - HALO, HALO), -1: (0, HALO)}
 LANDS = {0: HALO, 1: 0, -1: HALO + 16}
 SETS = 14
@@ -498,20 +498,21 @@
                 for k, value in enumerate(row_transform(d[2 * n : 2 * n + 4])):
                     x_ref[k, j, part, :] = value
 
-    def build_halo(step):
+    def build_halo(step, quarter):
         hx_ref = hx_refs[step % 2]
+        first = pl.multiple_of(8 * quarter, 8)
+        read = pl.multiple_of(jnp.minimum(8 * quarter, 16), 8)
         for dx in range(3):
             lanes = slice(dx * C, (dx + 1) * C)
-            d = [
+            both = [
                 time_mix(
-                    step,
-                    lambda frame, k=k: h_ref[frame, k % 2, pl.ds(k // 2, HALO_ROWS), lanes],
-                    F32,
+                    step, lambda frame, p=p: h_ref[frame, p, pl.ds(read, 16), lanes], F32
                 )
-                for k in range(4)
+                for p in range(2)
             ]
+            d = [both[0][:8], both[1][:8], both[0][1:9], both[1][1:9]]
             for k, value in enumerate(row_transform(d)):
-                hx_ref[k, :, lanes] = value.astype(BF)
+                hx_ref[k, pl.ds(first, 8), lanes] = value
 
     def settle(step, part):
         tau = step % 4
@@ -588,7 +589,7 @@
         x = [x_ref[k, j, :count, :] for j in range(4)]
         even, odd, both = [jnp.concatenate(part, axis=1) for part in (x[:3], x[1:], x)]
         if step < 8:
-            halo = hx_refs[step % 2][k]
+            halo = hx_refs[step % 2][k].astype(BF)
             even = jnp.concatenate([even, halo], axis=0)
             none = jnp.zeros((HALO_ROWS, C), BF)
             both = jnp.concatenate([both, jnp.concatenate([halo, none], axis=1)], axis=0)
@@ -619,9 +620,6 @@
         builds = step < 11
         settles = step > 0
         pieces = step < PIECES // QUARTERS
-        if builds and step < 7:
-            build(step + 1, I1 - 1)
-            build_halo(step + 1)
         if settles and step < 9:
             settle_halo(step - 1)
             settle_first(step - 1, I1 - 1)
@@ -639,6 +637,9 @@
             if step == 7:
                 for n in range(QUARTER):
                     build(8, jnp.maximum(QUARTER * k + n - 1, 0))
+            elif step < 7:
+                build(step + 1, QUARTER * k, QUARTER + 1)
+                build_halo(step + 1, k)
             elif builds:
                 build(step + 1, QUARTER * k, QUARTER)
             if pieces:
@@ -651,11 +652,13 @@
         if step == 7:
             build(8, I2 - 1)
 
-    @pl.loop(0, I1)
-    def _(i):
-        build(0, i)
-
-    build_halo(0)
+    @pl.loop(0, I1 // 4)
+    def _(block):
+        build(0, 4 * block, 5)
+
+    for quarter in range(QUARTERS):
+        build_halo(0, quarter)
+
     for step in range(12):
         run(step)
 
@@ -693,7 +696,7 @@
         scratch_shapes=[
             pltpu.VMEM((9, 38 * 16, CELLS), BF),
             pltpu.VMEM((6, R1, 4, SPAN, C), BF),
-            pltpu.VMEM((6, 2, HALO_ROWS + 8, K3), F32),
+            pltpu.VMEM((6, 2, HALO_ROWS, K3), F32),
             pltpu.VMEM((R2, 4, SPAN, C), BF),
             pltpu.VMEM((R2, 4, SPAN, C), BF),
             pltpu.VMEM((R2, 4, SPAN, C), BF),
@@ -701,8 +704,8 @@
             pltpu.VMEM((2, R1, COLS, C), BF),
             pltpu.VMEM((4, 4, I1 * SPAN, C), BF),
             pltpu.VMEM((4, 4, I1 * SPAN, C), BF),
-            pltpu.VMEM((4, HALO_ROWS, K3), BF),
-            pltpu.VMEM((4, HALO_ROWS, K3), BF),
+            pltpu.VMEM((4, HALO_ROWS, K3), F32),
+            pltpu.VMEM((4, HALO_ROWS, K3), F32),
             pltpu.VMEM((4, m1, C), F32),
             pltpu.VMEM((4, m1, C), F32),
             pltpu.VMEM((2, 2, m1, C), F32),

time: 84.3 us -> 86 us (1.020)
  Pallas kernels: 83.8 us -> 85.5 us
    pallas_call x1, Pallas kernels: 19.6 us -> 21.5 us  [gathered(): pl.pallas_call(gather_kernel, grid=(WEIGHT_STEPS,), in_specs=[pl.BlockSpe...]
where the time goes in v6:
time: 86 us; the launch traced here: 85.7 us
  Pallas kernels  85.5 us (99%)
    pallas_call x1, Pallas kernels, block_call(): pl.pallas_call(main_kernel, in_specs=[smem, vmem, vmem, vmem, vmem, hbm,...  64 us
    pallas_call x1, Pallas kernels, gathered(): pl.pallas_call(gather_kernel, grid=(WEIGHT_STEPS,), in_specs=[pl.BlockSpe...  21.5 us

profile of v6, /device:TPU:1, one launch (start us, length us, event | category | flops | bytes accessed | tf_op | source)
XLA Modules:
  0.0 85.7 jit_solution(2710865723299094058)
XLA Ops:
  0.0 21.5 %gather.1 = (bf16[4,2,22,16,128]{4,3,2,1,0:T(8,128)(2,1)}, bf16[14,3,384,384]{3,2,1,0:T(8,128)(2,1)}) custom-call(bf16[2,32,16,32]{3,2,1,0:T(8,128)(2,1)} %bitcast.9, bf16[3,3,3,384,384]{4,3,2,1,0:T(8,128)(2,1)} %w1_ref.1), custom_call_target="tpu_custom_call" | custom-call | flops 79626240 | bytes 36274176 | tf_op jit(solution)/shard_map/gather/pallas_call | solution.py:148
  21.5 64.0 %block.1 = (bf16[2,32,32,384]{3,2,1,0:T(8,128)(2,1)}, bf16[14,1152,384]{2,1,0:T(8,128)(2,1)}) custom-call(s32[9]{0:T(128)} %lengths.1, bf16[4,2,22,16,128]{4,3,2,1,0:T(8,128)(2,1)} %get-tuple-element.8.all_ref, bf16[432,384]{1,0:T(8,128)(2,1)} %bitcast.8, f32[384]{0:T(512)} %g1_ref.1, f32[384]{0:T(512)} %g2_ref.1, bf16[3,3,1152,384]{3,2,1,0:T(8,128)(2,1)} %bitcast.5, ...), custom_call_target="tpu_custom_call" | custom-call | tf_op jit(solution)/shard_map/block/pallas_call | solution.py:688
